TPU v7x, 512 devices: a whole 4x8x8 slice. The times are simulated.
512 devices in a mesh: tm: 128 (over z, y, core), rows: 4 (over x).
Axes of the slice: x: 4, y: 8, z: 8, core: 2. Of those that a mesh axis runs over, the one named last changes fastest.
Arguments:
- pivot_blocks: float32 [128, 512, 512], P('tm'), may hold values from -4 to 24, as said below
- lower_blocks: float32 [128, 512, 512], P('tm', None, 'rows'), may hold values from -5 to 0.5
- top_diagonal: float32 [128, 512, 512], P('tm', 'rows'), may hold values from -1 to 2, as said below
- top_coupling: float32 [128, 512, 512], P('tm', 'rows'), may hold values from -3 to 3
Outputs:
- sigma_diagonal: float32 [128, 512, 512], P('tm', 'rows')
- sigma_next: float32 [128, 512, 512], P('tm', 'rows')
- reduced_pivot: float32 [128, 512, 512], P('tm', 'rows')
Inputs may be any that keep to these rules, and one draw needn't show every extreme that they name: `pivot_blocks`: each block is symmetric, and the block-tridiagonal matrix with these diagonal blocks and the couplings lower_blocks is positive definite. `top_diagonal`: each block is symmetric.
All inputs are finite; a program needn't handle non-finite values.
Results may differ from a plain program's by a relative error of at most 0.0001.
Values sent between devices are 32-bit elements; how exact they have to be, the bound alone decides.
A program may use at most 64 MiB of HBM per device.

v0:
```python
import jax
import jax.numpy as jnp
from jax import lax
from jax.sharding import PartitionSpec as P

LEVELS = 2


precise = lax.Precision.HIGHEST


def passed_along(value, axis, steps):
    count = lax.axis_size(axis)
    leading, last = (max(0, -steps), min(count, count - steps))
    return lax.ppermute(value, axis, [(source, source + steps) for source in range(leading, last)])


def product(left, right):
    return jnp.dot(left, right, precision=precise, preferred_element_type=jnp.float32)


def product_flip(left, right):
    return lax.dot_general(
        left, right, (((1,), (1,)), ((), ())), precision=precise, preferred_element_type=jnp.float32
    )


def product_over(left, right):
    return lax.dot_general(
        left, right, (((0,), (0,)), ((), ())), precision=precise, preferred_element_type=jnp.float32
    )


def solve_with(factor, right_side):
    return jax.scipy.linalg.cho_solve((factor, True), right_side)


def local(pivot_blocks, lower_blocks, top_diagonal, top_coupling):
    parts_count = lax.axis_size("tm")
    position = lax.axis_index("tm")
    row_part = lax.axis_index("rows")
    full_width = pivot_blocks.shape[1]
    quarter = lower_blocks.shape[2]
    row_start = row_part * quarter
    first_pivot = pivot_blocks[0]
    lower_columns = jnp.where(position == 0, jnp.zeros_like(lower_blocks[0]), lower_blocks[0])
    lower_rows = lax.all_to_all(lower_columns, "rows", split_axis=0, concat_axis=1, tiled=True)
    next_rows = passed_along(lower_rows, "tm", -1)
    upper_columns = next_rows.T
    pivot_rows = lax.dynamic_slice_in_dim(first_pivot, row_start, quarter, 0)
    unit_columns = (
        jnp.arange(full_width)[:, None] == row_start + jnp.arange(quarter)[None, :]
    ).astype(jnp.float32)
    saved = []
    for tier_index in range(LEVELS):
        spacing = 2**tier_index
        if tier_index == 0:
            whole_pivot = first_pivot
        else:
            whole_pivot = lax.all_gather(pivot_rows, "rows", axis=0, tiled=True)
        factor = jnp.linalg.cholesky(whole_pivot)
        solved = solve_with(
            factor, jnp.concatenate([lower_columns, upper_columns, unit_columns], axis=1)
        )
        left_columns = solved[:, :quarter]
        right_columns = solved[:, quarter : 2 * quarter]
        inverse_columns = solved[:, 2 * quarter :]
        left_solved, right_solved = (
            lax.all_gather(left_columns, "rows", axis=1, tiled=True),
            lax.all_gather(right_columns, "rows", axis=1, tiled=True),
        )
        drop_left = product_over(lower_columns, left_solved)
        upper_new = -product_over(upper_columns, left_solved)
        left_bound = passed_along(jnp.stack([drop_left, upper_new]), "tm", -spacing)
        drop_right = product_over(upper_columns, right_solved)
        lower_new = -product_over(lower_columns, right_solved)
        right_bound = passed_along(jnp.stack([drop_right, lower_new]), "tm", spacing)
        pivot_rows = pivot_rows - left_bound[0] - right_bound[0]
        upper_columns = left_bound[1].T
        lower_columns = right_bound[1].T
        saved.append((left_solved, right_solved, inverse_columns))
    diagonal_rows = top_diagonal[0]
    coupling_rows = jnp.where(
        position + 2**LEVELS >= parts_count, jnp.zeros_like(top_coupling[0]), top_coupling[0]
    )
    for tier_index in reversed(range(LEVELS)):
        spacing = 2**tier_index
        saved_left, saved_right, saved_inverse = saved[tier_index]
        left_rows = lax.dynamic_slice_in_dim(saved_left, row_start, quarter, 0)
        right_rows = lax.dynamic_slice_in_dim(saved_right, row_start, quarter, 0)
        gathered = lax.all_gather(
            jnp.stack([diagonal_rows, coupling_rows]), "rows", axis=1, tiled=True
        )
        from_left = passed_along(gathered, "tm", spacing)
        far_diagonal = passed_along(gathered[0], "tm", -spacing)
        near_diagonal = from_left[0]
        near_next = from_left[1]
        cross_near = product(left_rows, near_diagonal) + product_flip(right_rows, near_next)
        cross_far = product(left_rows, near_next) + product(right_rows, far_diagonal)
        diagonal_rows = (
            saved_inverse.T
            + product_flip(cross_near, saved_left)
            + product_flip(cross_far, saved_right)
        )
        coupling_rows = -cross_far
    coupling_rows = jnp.where(
        position == parts_count - 1, jnp.zeros_like(coupling_rows), coupling_rows
    )
    return (diagonal_rows[None], coupling_rows[None], pivot_rows[None])


def solution(mesh):
    placed = (
        P("tm", None, None),
        P("tm", None, "rows"),
        P("tm", "rows", None),
        P("tm", "rows", None),
    )
    return jax.shard_map(
        local,
        mesh=mesh,
        in_specs=placed,
        out_specs=(P("tm", "rows", None), P("tm", "rows", None), P("tm", "rows", None)),
        check_vma=False,
    )
```

profile of v0, /device:TPU:1, one launch (start us, length us, event | category | flops | bytes accessed | tf_op | source)
XLA Modules:
  0.0 628.3 jit_solution(3669851343186253407)
XLA Ops:
  9.1 4.8 all-to-all-start
  14.5 11.7 %cholesky.286 = f32[128,128]{1,0:T(8,128)S(1)} custom-call(f32[128,128]{1,0:T(8,128)S(1)} %cholesky.426), custom_call_target="Cholesky" | custom-call | tf_op jit(solution)/shard_map/jit(cholesky)/cholesky | solution.py:61
  26.3 9.8 %custom-call.29 = f32[1,128,128]{1,2,0:T(8,128)S(1)} custom-call(f32[1,128,128]{2,1,0:T(8,128)S(1)} %get-tuple-element.70), custom_call_target="InvertDiagBlocksLowerTriangular" | custom-call | tf_op jit(solution)/shard_map/jit(cholesky)/cholesky | solution.py:61
  37.6 11.7 %cholesky.305 = f32[128,128]{1,0:T(8,128)S(1)} custom-call(f32[128,128]{1,0:T(8,128)S(1)} %cholesky.430), custom_call_target="Cholesky" | custom-call | tf_op jit(solution)/shard_map/jit(cholesky)/cholesky | solution.py:61
  49.3 10.2 %custom-call.30 = f32[1,128,128]{1,2,0:T(8,128)S(1)} custom-call(f32[1,128,128]{2,1,0:T(8,128)S(1)} %get-tuple-element.67), custom_call_target="InvertDiagBlocksLowerTriangular" | custom-call | tf_op jit(solution)/shard_map/jit(cholesky)/cholesky | solution.py:61
  61.7 13.2 %cholesky.326 = f32[128,128]{1,0:T(8,128)} custom-call(f32[128,128]{1,0:T(8,128)} %cholesky.435), custom_call_target="Cholesky" | custom-call | tf_op jit(solution)/shard_map/jit(cholesky)/cholesky | solution.py:61
  77.1 11.3 %custom-call.31 = f32[1,128,128]{1,2,0:T(8,128)} custom-call(f32[1,128,128]{2,1,0:T(8,128)} %get-tuple-element.64), custom_call_target="InvertDiagBlocksLowerTriangular" | custom-call | tf_op jit(solution)/shard_map/jit(cholesky)/cholesky | solution.py:61
  89.8 11.7 %cholesky.343 = f32[128,128]{1,0:T(8,128)S(1)} custom-call(f32[128,128]{1,0:T(8,128)S(1)} %convolution_subtract_fusion.14), custom_call_target="Cholesky" | custom-call | tf_op jit(solution)/shard_map/jit(cholesky)/cholesky | solution.py:61
  105.8 8.0 %while.4 = (s32[]{:T(128)}, f32[512,512]{1,0:T(8,128)S(1)}, s32[4,2]{0,1:T(2,128)S(1)}, f32[4,128,128]{2,1,0:T(8,128)S(1)}, s32[]{:T(128)}) while((s32[]{:T(128)}, f32[512,512]{1,0:T(8,128)S(1)}, s32[4,2]{0,1:T(2,128)S(1)}, f32[4,128,128]{2,1,0:T(8,128)S(1)}, s32[]{:T(128)}) %tuple.60), condition=%wide.while_cond, body=%wide.while_body.sunk | while | flops 2 | bytes 131181 | solution.py:35
  113.8 7.0 %collective-permute-start = (f32[128,512]{0,1:T(8,128)}, f32[128,512]{0,1:T(8,128)S(1)}, u32[]{:S(2)}, u32[]{:S(2)}) collective-permute-start(f32[128,512]{0,1:T(8,128)} %bitcast.13), channel_id=1, source_target_pairs={{4,0},{8,4},{12,8},{16,12},{20,16},{24,20},{28,24},{32,28},{36,32}... | collective-permute-start | bytes 786440 | tf_op jit(solution)/shard_map/ppermute | solution.py:15
  120.9 39.3 %custom-call.32 = f32[4,128,128]{1,2,0:T(8,128)S(1)} custom-call(f32[4,128,128]{2,1,0:T(8,128)S(1)} %get-tuple-element.19), custom_call_target="InvertDiagBlocksLowerTriangular" | custom-call | tf_op jit(solution)/shard_map/jit(_cho_solve)/triangular_solve | solution.py:35
  169.3 30.1 %all-gather.9.cloned.1.call-done = f32[512,512]{1,0:T(8,128)} async-done(((f32[512,128]{1,0:T(8,128)}), f32[512,512]{1,0:T(8,128)}) %all-gather.9.cloned.1.call-update) | async-done | bytes 1048592 | tf_op jit(solution)/shard_map/all_gather | solution.py:69
  208.7 25.7 %all-gather.11.cloned.1.call-done = f32[512,512]{1,0:T(8,128)} async-done(((f32[512,128]{1,0:T(8,128)}), f32[512,512]{1,0:T(8,128)}) %all-gather.11.cloned.1.call-update) | async-done | bytes 1048592 | tf_op jit(solution)/shard_map/all_gather | solution.py:70
  240.2 4.5 collective-permute-start.2
  244.8 6.4 %collective-permute-done.2 = f32[2,128,512]{1,2,0:T(8,128)} collective-permute-done((f32[2,128,512]{1,2,0:T(8,128)}, f32[2,128,512]{1,2,0:T(8,128)}, u32[]{:S(2)}, u32[]{:S(2)}) %collective-permute-start.2) | collective-permute-done | bytes 524320 | tf_op jit(solution)/shard_map/ppermute | solution.py:15
  257.6 29.1 %all-gather.21.cloned.1.call-done = f32[1,512,512]{1,2,0:T(8,128)} async-done(((f32[1,128,512]{1,2,0:T(8,128)}), f32[1,512,512]{1,2,0:T(8,128)}) %all-gather.21.cloned.1.call-update) | async-done | bytes 1048592 | tf_op jit(solution)/shard_map/all_gather | solution.py:60
  291.8 11.7 %cholesky.358 = f32[128,128]{1,0:T(8,128)S(1)} custom-call(f32[128,128]{1,0:T(8,128)S(1)} %cholesky.439), custom_call_target="Cholesky" | custom-call | tf_op jit(solution)/shard_map/jit(cholesky)/cholesky | solution.py:61
  303.7 9.8 %custom-call.33 = f32[1,128,128]{1,2,0:T(8,128)S(1)} custom-call(f32[1,128,128]{2,1,0:T(8,128)S(1)} %get-tuple-element.60), custom_call_target="InvertDiagBlocksLowerTriangular" | custom-call | tf_op jit(solution)/shard_map/jit(cholesky)/cholesky | solution.py:61
  316.0 11.7 %cholesky.377 = f32[128,128]{1,0:T(8,128)S(1)} custom-call(f32[128,128]{1,0:T(8,128)S(1)} %cholesky.443), custom_call_target="Cholesky" | custom-call | tf_op jit(solution)/shard_map/jit(cholesky)/cholesky | solution.py:61
  329.1 9.9 %custom-call.34 = f32[1,128,128]{1,2,0:T(8,128)S(1)} custom-call(f32[1,128,128]{2,1,0:T(8,128)S(1)} %get-tuple-element.57), custom_call_target="InvertDiagBlocksLowerTriangular" | custom-call | tf_op jit(solution)/shard_map/jit(cholesky)/cholesky | solution.py:61
  340.6 11.7 %cholesky.398 = f32[128,128]{1,0:T(8,128)S(1)} custom-call(f32[128,128]{1,0:T(8,128)S(1)} %cholesky.448), custom_call_target="Cholesky" | custom-call | tf_op jit(solution)/shard_map/jit(cholesky)/cholesky | solution.py:61
  353.1 9.8 %custom-call.35 = f32[1,128,128]{1,2,0:T(8,128)S(1)} custom-call(f32[1,128,128]{2,1,0:T(8,128)S(1)} %get-tuple-element.54), custom_call_target="InvertDiagBlocksLowerTriangular" | custom-call | tf_op jit(solution)/shard_map/jit(cholesky)/cholesky | solution.py:61
  364.3 11.7 %cholesky.415 = f32[128,128]{1,0:T(8,128)S(1)} custom-call(f32[128,128]{1,0:T(8,128)S(1)} %convolution_subtract_fusion.13), custom_call_target="Cholesky" | custom-call | tf_op jit(solution)/shard_map/jit(cholesky)/cholesky | solution.py:61
  381.3 14.4 %while.5 = (s32[]{:T(128)}, f32[512,512]{1,0:T(8,128)}, s32[4,2]{0,1:T(2,128)S(1)}, f32[4,128,128]{2,1,0:T(8,128)}, s32[]{:T(128)}) while((s32[]{:T(128)}, f32[512,512]{1,0:T(8,128)}, s32[4,2]{0,1:T(2,128)S(1)}, f32[4,128,128]{2,1,0:T(8,128)}, s32[]{:T(128)}) %tuple.80), condition=%wide.while_cond.clone, body=%wide.while_body.clone.sunk | while | flops 2 | bytes 132705 | solution.py:35
  395.7 40.2 %custom-call.36 = f32[4,128,128]{1,2,0:T(8,128)S(1)} custom-call(f32[4,128,128]{2,1,0:T(8,128)} %get-tuple-element.20), custom_call_target="InvertDiagBlocksLowerTriangular" | custom-call | tf_op jit(solution)/shard_map/jit(_cho_solve)/triangular_solve | solution.py:35
  447.2 4.4 collective-permute-start.3
  454.7 23.1 %collective-permute-done.4 = f32[512,512]{1,0:T(8,128)} collective-permute-done((f32[512,512]{1,0:T(8,128)S(1)}, f32[512,512]{1,0:T(8,128)}, u32[]{:S(2)}, u32[]{:S(2)}) %collective-permute-start.4) | collective-permute-done | bytes 1048608 | tf_op jit(solution)/shard_map/ppermute | solution.py:15
  482.6 11.3 %collective-permute-done.3 = f32[2,512,512]{2,1,0:T(8,128)} collective-permute-done((f32[2,512,512]{2,1,0:T(8,128)}, f32[2,512,512]{2,1,0:T(8,128)}, u32[]{:S(2)}, u32[]{:S(2)}) %collective-permute-start.3) | collective-permute-done | bytes 2097184 | tf_op jit(solution)/shard_map/ppermute | solution.py:15
  494.0 20.3 %all-gather.13.cloned.1.call-done = f32[512,512]{1,0:T(8,128)} async-done(((f32[512,128]{1,0:T(8,128)}), f32[512,512]{1,0:T(8,128)}) %all-gather.13.cloned.1.call-update) | async-done | bytes 1048592 | tf_op jit(solution)/shard_map/all_gather | solution.py:69
  525.7 41.0 %all-gather.19.cloned.1.call-done = f32[2,512,512]{1,2,0:T(8,128)} async-done(((f32[2,128,512]{1,2,0:T(8,128)}), f32[2,512,512]{1,2,0:T(8,128)}) %all-gather.19.cloned.1.call-update) | async-done | bytes 2097168 | tf_op jit(solution)/shard_map/all_gather | solution.py:91
  566.7 4.7 collective-permute-start.5
  594.4 11.4 %collective-permute-done.8 = f32[2,128,512]{1,2,0:T(8,128)S(1)} collective-permute-done((f32[2,128,512]{1,2,0:T(8,128)S(1)}, f32[2,128,512]{1,2,0:T(8,128)S(1)}, u32[]{:S(2)}, u32[]{:S(2)}) %collective-permute-start.8) | collective-permute-done | bytes 524320 | tf_op jit(solution)/shard_map/ppermute | solution.py:15
  (210 shorter events, 148.4 us)
Async XLA Ops:
  7.2 6.8 %copy-start.6 = (f32[1,512,512]{2,1,0:T(8,128)S(1)}, f32[1,512,512]{2,1,0:T(8,128)}, u32[]{:S(2)}) copy-start(f32[1,512,512]{2,1,0:T(8,128)} %param.7) | copy-start | bytes 3145732
  9.1 104.7 %all-to-all-start = ((f32[4,128,128]{1,2,0:T(8,128)}), f32[4,128,128]{1,2,0:T(8,128)}, u32[]{:S(2)}, u32[]{:S(2)}) async-start(f32[4,128,128]{1,2,0:T(8,128)} %copy.9), calls=%async_computation | async-start | bytes 524288 | tf_op jit(solution)/shard_map/all_to_all | solution.py:47
  13.9 185.5 %all-gather.9.cloned.1.call-start = ((), (), s32[]{:S(2)}) async-start(), calls=%async_computation.1 | async-start | bytes 1310720 | tf_op jit(solution)/shard_map/all_gather | solution.py:69
  113.8 47.4 %collective-permute-start = (f32[128,512]{0,1:T(8,128)}, f32[128,512]{0,1:T(8,128)S(1)}, u32[]{:S(2)}, u32[]{:S(2)}) collective-permute-start(f32[128,512]{0,1:T(8,128)} %bitcast.13), channel_id=1, source_target_pairs={{4,0},{8,4},{12,8},{16,12},{20,16},{24,20},{28,24},{32,28},{36,32}... | collective-permute-start | bytes 786440 | tf_op jit(solution)/shard_map/ppermute | solution.py:15
  120.9 40.3 %copy-start.12 = (f32[512,128]{1,0:T(8,128)}, f32[512,128]{1,0:T(8,128)S(1)}, u32[]{:S(2)}) copy-start(f32[512,128]{1,0:T(8,128)S(1)} %fusion.50) | copy-start | bytes 786436
  167.2 32.3 %copy-start.15 = (f32[128,512]{0,1:T(8,128)S(1)}, f32[128,512]{0,1:T(8,128)}, u32[]{:S(2)}) copy-start(f32[128,512]{0,1:T(8,128)} %copy-done.14) | copy-start | bytes 786436
  168.5 65.9 %all-gather.11.cloned.1.call-start = ((), (), s32[]{:S(2)}) async-start(), calls=%async_computation.2 | async-start | bytes 1310720 | tf_op jit(solution)/shard_map/all_gather | solution.py:70
  169.3 117.5 %all-gather.21.cloned.1.call-start = ((), (), s32[]{:S(2)}) async-start(), calls=%async_computation.7 | async-start | bytes 1310720 | tf_op jit(solution)/shard_map/all_gather | solution.py:60
  199.4 3.1 copy-start
  205.3 39.5 %collective-permute-start.1 = (f32[2,128,512]{1,2,0:T(8,128)}, f32[2,128,512]{1,2,0:T(8,128)}, u32[]{:S(2)}, u32[]{:S(2)}) collective-permute-start(f32[2,128,512]{1,2,0:T(8,128)} %pad_maximum_fusion.4), channel_id=1, source_target_pairs={{4,0},{8,4},{12,8},{16,12},{20,16},{24,20},{28,24},{32,28},{36,32}... | collective-permute-start | bytes 1572872 | tf_op jit(solution)/shard_map/ppermute | solution.py:15
  234.4 3.2 copy-start.1
  240.2 11.0 %collective-permute-start.2 = (f32[2,128,512]{1,2,0:T(8,128)}, f32[2,128,512]{1,2,0:T(8,128)}, u32[]{:S(2)}, u32[]{:S(2)}) collective-permute-start(f32[2,128,512]{1,2,0:T(8,128)} %pad_maximum_fusion.5), channel_id=1, source_target_pairs={{0,4},{4,8},{8,12},{12,16},{16,20},{20,24},{24,28},{28,32},{32,36}... | collective-permute-start | bytes 1572872 | tf_op jit(solution)/shard_map/ppermute | solution.py:15
  244.8 11.9 %copy-start.13 = (f32[512,128]{1,0:T(8,128)S(1)}, f32[512,128]{1,0:T(8,128)}, u32[]{:S(2)}) copy-start(f32[512,128]{1,0:T(8,128)} %copy-done.12) | copy-start | bytes 786436
  253.3 3.4 copy-start.16
  253.3 3.4 copy-start.17
  253.3 193.8 %all-gather.15.cloned.1.call-start = ((), (), s32[]{:S(2)}) async-start(), calls=%async_computation.4 | async-start | bytes 2621440 | tf_op jit(solution)/shard_map/all_gather | solution.py:91
  256.2 223.3 %all-gather.17.cloned.1.call-start = ((), (), s32[]{:S(2)}) async-start(), calls=%async_computation.5 | async-start | bytes 1310720 | tf_op jit(solution)/shard_map/all_gather | solution.py:70
  286.7 2.6 copy-start.7
  395.7 45.0 %copy-start.5 = (f32[512,512]{1,0:T(8,128)S(1)}, f32[512,512]{1,0:T(8,128)}, u32[]{:S(2)}) copy-start(f32[512,512]{1,0:T(8,128)} %get-tuple-element.176) | copy-start | bytes 3145732
  447.1 67.1 %all-gather.13.cloned.1.call-start = ((), (), s32[]{:S(2)}) async-start(), calls=%async_computation.3 | async-start | bytes 1310720 | tf_op jit(solution)/shard_map/all_gather | solution.py:69
  447.2 46.8 %collective-permute-start.3 = (f32[2,512,512]{2,1,0:T(8,128)}, f32[2,512,512]{2,1,0:T(8,128)}, u32[]{:S(2)}, u32[]{:S(2)}) collective-permute-start(f32[2,512,512]{2,1,0:T(8,128)} %all-gather.15.cloned.1.call-done), channel_id=1, source_target_pairs={{0,8},{4,12},{8,16},{12,20},{16,24},{20,28},{24,32},{28,36},{32,40... | collective-permute-start | bytes 6291464 | tf_op jit(solution)/shard_map/ppermute | solution.py:15
  451.6 115.1 %all-gather.19.cloned.1.call-start = ((), (), s32[]{:S(2)}) async-start(), calls=%async_computation.6 | async-start | bytes 2621440 | tf_op jit(solution)/shard_map/all_gather | solution.py:91
  452.9 24.8 %collective-permute-start.4 = (f32[512,512]{1,0:T(8,128)S(1)}, f32[512,512]{1,0:T(8,128)}, u32[]{:S(2)}, u32[]{:S(2)}) collective-permute-start(f32[512,512]{1,0:T(8,128)S(1)} %slice_bitcast_fusion.4), channel_id=1, source_target_pairs={{8,0},{12,4},{16,8},{20,12},{24,16},{28,20},{32,24},{36,28},{40,32... | collective-permute-start | bytes 3145736 | tf_op jit(solution)/shard_map/ppermute | solution.py:15
  479.4 38.0 %copy-start.2 = (f32[512,512]{1,0:T(8,128)S(1)}, f32[512,512]{1,0:T(8,128)}, u32[]{:S(2)}) copy-start(f32[512,512]{1,0:T(8,128)} %all-gather.17.cloned.1.call-done) | copy-start | bytes 3145732
  514.2 5.6 copy-start.3
  566.7 7.8 %copy-start.4 = (f32[512,512]{1,0:T(8,128)S(1)}, f32[512,512]{1,0:T(8,128)}, u32[]{:S(2)}) copy-start(f32[512,512]{1,0:T(8,128)} %all-gather.13.cloned.1.call-done) | copy-start | bytes 3145732
  566.7 43.3 %collective-permute-start.5 = (f32[2,512,512]{1,2,0:T(8,128)}, f32[2,512,512]{1,2,0:T(8,128)}, u32[]{:S(2)}, u32[]{:S(2)}) collective-permute-start(f32[2,512,512]{1,2,0:T(8,128)} %all-gather.19.cloned.1.call-done), channel_id=1, source_target_pairs={{0,4},{4,8},{8,12},{12,16},{16,20},{20,24},{24,28},{28,32},{32,36}... | collective-permute-start | bytes 6291464 | tf_op jit(solution)/shard_map/ppermute | solution.py:15
  574.5 8.0 %copy-start.19 = (f32[2,512,512]{1,2,0:T(8,128)S(1)}, f32[2,512,512]{1,2,0:T(8,128)}, u32[]{:S(2)}) copy-start(f32[2,512,512]{1,2,0:T(8,128)} %all-gather.19.cloned.1.call-done) | copy-start | bytes 6291460
  578.3 16.1 %collective-permute-start.7 = (f32[2,128,512]{1,2,0:T(8,128)}, f32[2,128,512]{1,2,0:T(8,128)}, u32[]{:S(2)}, u32[]{:S(2)}) collective-permute-start(f32[2,128,512]{1,2,0:T(8,128)} %pad_maximum_fusion.8), channel_id=1, source_target_pairs={{8,0},{12,4},{16,8},{20,12},{24,16},{28,20},{32,24},{36,28},{40,32... | collective-permute-start | bytes 1572872 | tf_op jit(solution)/shard_map/ppermute | solution.py:15
  582.6 23.2 %copy-start.11 = (f32[1,128,512]{1,2,0:T(8,128)S(1)}, f32[1,128,512]{1,2,0:T(8,128)}, u32[]{:S(2)}) copy-start(f32[1,128,512]{1,2,0:T(8,128)} %get-tuple-element.48) | copy-start | bytes 786436
  583.6 24.0 %collective-permute-start.6 = (f32[512,512]{0,1:T(8,128)}, f32[512,512]{0,1:T(8,128)}, u32[]{:S(2)}, u32[]{:S(2)}) collective-permute-start(f32[512,512]{0,1:T(8,128)} %slice_bitcast_fusion), channel_id=1, source_target_pairs={{4,0},{8,4},{12,8},{16,12},{20,16},{24,20},{28,24},{32,28},{36,32}... | collective-permute-start | bytes 3145736 | tf_op jit(solution)/shard_map/ppermute | solution.py:15
  588.4 17.4 %collective-permute-start.8 = (f32[2,128,512]{1,2,0:T(8,128)S(1)}, f32[2,128,512]{1,2,0:T(8,128)S(1)}, u32[]{:S(2)}, u32[]{:S(2)}) collective-permute-start(f32[2,128,512]{1,2,0:T(8,128)S(1)} %pad_maximum_fusion.9), channel_id=1, source_target_pairs={{0,8},{4,12},{8,16},{12,20},{16,24},{20,28},{24,32},{28,36},{32,40... | collective-permute-start | bytes 1572872 | tf_op jit(solution)/shard_map/ppermute | solution.py:15
  (5 other events, 5.1 us)
Sparse Core Ops, SparseCore 0:
  168.6 30.7 all-gather.8
  202.1 32.2 all-gather.10
  253.4 33.2 all-gather.20
  288.7 38.5 all-gather.14
  447.2 32.1 all-gather.16
  482.0 32.2 all-gather.12
  525.8 40.8 all-gather.18
where the time goes:
time: 641 us; the launch traced here: 628 us
  other arithmetic  259 us (40%)
  waiting for transfers between devices  203 us (32%)
  matrix products  71 us (11%)
  starting transfers between devices  38.6 us (6%)
  local copies, waits for them, and re-layouts  36.9 us (6%)
  between operations  20.3 us (3%)
    another operation x29, other arithmetic, local(): factor = jnp.linalg.cholesky(whole_pivot)  163 us
    another operation x7, other arithmetic, solve_with(): return jax.scipy.linalg.cho_solve((factor, True), right_side)  81 us
    ppermute x9, waiting for transfers between devices, passed_along(): lax.ppermute(value, axis, [(source, source + steps) for source in range(l...  54.2 us
    all_gather x2, waiting for transfers between devices, local(): lax.all_gather(left_columns, 'rows', axis=1, tiled=True)  50.4 us
    all_gather x2, waiting for transfers between devices, local(): lax.all_gather(jnp.stack([diagonal_rows, coupling_rows]), 'rows', axis=1,...  41 us
    ppermute x9, starting transfers between devices, passed_along(): lax.ppermute(value, axis, [(source, source + steps) for source in range(l...  33.1 us
    all_gather x1, waiting for transfers between devices, local(): whole_pivot = lax.all_gather(pivot_rows, 'rows', axis=0, tiled=True)  29.1 us
    all_gather x2, waiting for transfers between devices, local(): lax.all_gather(right_columns, 'rows', axis=1, tiled=True)  27.3 us
  transfers between devices with their start and end apart: 17, of which 11 were waited for; matrix products, arithmetic and copies ran while one was open for 53% of the time, Pallas kernels for 0%

commit v1 on v0

v1 whole, which is shorter than its diff:
```python
import functools

import jax
import jax.numpy as jnp
from jax import lax
from jax.experimental import pallas as pl
from jax.experimental.pallas import tpu as pltpu
from jax.sharding import PartitionSpec as P

f32 = jnp.float32
bf16 = jnp.bfloat16
MESH = pl.DeviceIdType.MESH
VMEM = pl.BlockSpec(memory_space=pltpu.VMEM)
LIMIT = 56 * 2**20


def dot(a, b, flip=False, precision=None):
    dims = (((1,), (1 if flip else 0,)), ((), ()))
    return lax.dot_general(a, b, dims, precision=precision, preferred_element_type=f32)


def split(x):
    high = x.astype(bf16)
    return high, (x - high.astype(f32)).astype(bf16)


def dot3(a, b, flip=False):
    ah, al = split(a)
    bh, bl = split(b)
    return dot(ah, bh, flip) + (dot(ah, bl, flip) + dot(al, bh, flip))


def dot1(a, b):
    return dot(a.astype(bf16), b.astype(bf16))


def full_dot(a, b):
    return dot(a, b, precision=lax.Precision.HIGHEST)


def eye(size):
    rows = lax.broadcasted_iota(jnp.int32, (size, size), 0)
    columns = lax.broadcasted_iota(jnp.int32, (size, size), 1)
    return rows == columns


def scales(pivot):
    only = jnp.where(eye(pivot.shape[0]), pivot, 0.0)
    return (
        lax.rsqrt(jnp.sum(only, axis=1, keepdims=True)),
        lax.rsqrt(jnp.sum(only, axis=0, keepdims=True)),
    )


def row_norm(x):
    return jnp.max(jnp.sum(jnp.abs(x), axis=1, keepdims=True), axis=0, keepdims=True)


def newton_start(pivot, x_ref, steps):
    column, row = scales(pivot)
    scaled = pivot * column * row
    factor = jnp.minimum(1.0, 1.9 / row_norm(scaled))
    one = jnp.where(eye(pivot.shape[0]), 1.0, 0.0)
    rest = one - factor * scaled
    x = factor * (one + rest)
    for _ in range(steps):
        rest = dot1(rest, rest)
        x = x + dot1(x, rest)
    x_ref[...] = x


def finish_kernel(pivot_ref, x_ref, out_ref, a_ref):
    size = pivot_ref.shape[0]
    column, row = scales(pivot_ref[...])
    a_ref[...] = pivot_ref[...] * column * row

    def one():
        return jnp.where(eye(size), 1.0, 0.0)

    x = x_ref[...]
    rest = one() - dot3(a_ref[...], x)
    first = row_norm(rest)[0, 0]
    out_ref[...] = x + dot1(x, rest)

    @pl.when(jnp.logical_not(first < 2.0**-7))
    def _():
        @pl.when(jnp.logical_not(first < 0.5))
        def _():
            out_ref[...] = one() / row_norm(a_ref[...])

        def more(state):
            count, norm = state
            return jnp.logical_and(count < 60, jnp.logical_not(norm < 1e-3))

        def step(state):
            count, _ = state
            rest = one() - full_dot(a_ref[...], out_ref[...])
            out_ref[...] = out_ref[...] + full_dot(out_ref[...], rest)
            return count + 1, row_norm(rest)[0, 0]

        lax.while_loop(more, step, (0, jnp.float32(1.0)))

    out_ref[...] = out_ref[...] * column * row


def finish(pivot, x):
    size = pivot.shape[0]
    return pl.pallas_call(
        finish_kernel,
        out_shape=jax.ShapeDtypeStruct((size, size), f32),
        in_specs=[VMEM] * 2,
        out_specs=VMEM,
        scratch_shapes=[pltpu.VMEM((size, size), f32)],
        compiler_params=pltpu.CompilerParams(vmem_limit_bytes=LIMIT),
    )(pivot, x)


class Sender:
    def __init__(self, parts, send_sems, recv_sems):
        self.parts, self.send_sems, self.recv_sems = parts, send_sems, recv_sems
        self.count = 0
        self.part = lax.axis_index("tm")
        self.row = lax.axis_index("rows")
        self.copies = []

    def device(self, parts=0, rows=0):
        return (
            lax.rem(self.part + (parts + self.parts), self.parts),
            lax.rem(self.row + (rows + 4), 4),
        )

    def greet(self, *offsets):
        barrier = pltpu.get_barrier_semaphore()
        for parts, rows in offsets:
            pl.semaphore_signal(barrier, inc=1, device_id=self.device(parts, rows), device_id_type=MESH)
        pl.semaphore_wait(barrier, len(offsets))

    def send(self, source, target, parts=0, rows=0):
        copy = pltpu.make_async_remote_copy(
            src_ref=source,
            dst_ref=target,
            send_sem=self.send_sems.at[self.count],
            recv_sem=self.recv_sems.at[self.count],
            device_id=self.device(parts, rows),
            device_id_type=MESH,
        )
        self.count += 1
        copy.start()
        self.copies.append(copy)
        return copy

    def sent(self):
        for copy in self.copies:
            copy.wait_send()


class Ring:
    def __init__(self, sender, view):
        self.sender, self.view = sender, view
        row = sender.row
        self.left = lax.rem(row + 3, 4)
        self.right = lax.rem(row + 1, 4)
        self.far = lax.rem(row + 2, 4)
        self.first = sender.send(view(row), view(row), rows=1)
        self.second = sender.send(view(row), view(row), rows=-1)

    def forward(self):
        self.first.wait_recv()
        self.third = self.sender.send(self.view(self.left, 0), self.view(self.left, 0), rows=1)
        self.second.wait_recv()
        self.fourth = self.sender.send(self.view(self.right, 1), self.view(self.right, 1), rows=-1)

    def done(self):
        self.third.wait_recv()
        self.fourth.wait_recv()


def columns_of(ref):
    quarter = ref.shape[1] // 4
    half = ref.shape[0] // 2

    def view(q, h=None):
        rows = slice(None) if h is None else pl.ds(h * half, half)
        return ref.at[rows, pl.ds(pl.multiple_of(q * quarter, quarter), quarter)]

    return view


def rows_of(ref):
    quarter = ref.shape[0] // 4
    half = quarter // 2

    def view(q, h=None):
        if h is None:
            return ref.at[pl.ds(pl.multiple_of(q * quarter, quarter), quarter), :]
        return ref.at[pl.ds(pl.multiple_of(q * quarter + h * half, half), half), :]

    return view


def first_kernel(
    parts, pivot_ref, lower_ref, s_ref, w_ref,
    v_ref, next_ref, x_ref, sd_ref, wd_ref, su_ref,
    w_masked, send_sems, recv_sems,
):
    sender = Sender(parts, send_sems, recv_sems)
    part, row = sender.part, sender.row
    quarter = lower_ref.shape[1]
    own = pl.ds(pl.multiple_of(row * quarter, quarter), quarter)
    v_ref[:, own] = jnp.where(part == 0, 0.0, lower_ref[...])
    w_masked[...] = jnp.where(part + 4 >= parts, 0.0, w_ref[...])
    sender.greet((0, 1), (0, -1), (1, 0), (-1, 0), (2, 0), (-2, 0))
    view, target = columns_of(v_ref), columns_of(next_ref)
    ring = Ring(sender, view)
    arriving = [sender.send(view(row), target(row), parts=-1)]
    arriving.append(sender.send(w_masked, wd_ref, parts=2))
    arriving.append(sender.send(s_ref, sd_ref, parts=2))

    newton_start(pivot_ref[...], x_ref, 2)

    ring.forward()
    arriving.append(sender.send(view(ring.left), target(ring.left), parts=-1))
    arriving.append(sender.send(view(ring.right), target(ring.right), parts=-1))
    arriving.append(sender.send(s_ref, su_ref, parts=-2))
    ring.third.wait_recv()
    arriving.append(sender.send(view(ring.far, 0), target(ring.far, 0), parts=-1))
    ring.fourth.wait_recv()
    arriving.append(sender.send(view(ring.far, 1), target(ring.far, 1), parts=-1))
    for copy in arriving:
        copy.wait_recv()
    sender.sent()


def second_kernel(
    parts, pivot_ref, g_ref, v_ref, next_ref, sdq_ref, wdq_ref, suq_ref,
    d2_ref, x_ref, v2_ref, u2_ref, left_ref, right_ref, above_left, above_right, below_right,
    sd_ref, wd_ref, su_ref,
    g_below, g_above, v_below, v_above, z_ref, y_ref, send_sems, recv_sems,
):
    sender = Sender(parts, send_sems, recv_sems)
    row = sender.row
    quarter = suq_ref.shape[0]
    own = pl.ds(pl.multiple_of(row * quarter, quarter), quarter)
    sender.greet((0, 1), (0, -1), (1, 0), (-1, 0))
    from_below = sender.send(g_ref, g_below, parts=1)
    from_above = sender.send(g_ref, g_above, parts=-1)
    wd_ref[own, :] = wdq_ref[...]
    sd_ref[own, :] = sdq_ref[...]
    su_ref[own, :] = suq_ref[...]
    ring_w = Ring(sender, rows_of(wd_ref))
    ring_d = Ring(sender, rows_of(sd_ref))
    ring_u = Ring(sender, rows_of(su_ref))
    v_from_below = sender.send(v_ref, v_below, parts=1)
    v_from_above = sender.send(next_ref, v_above, parts=-1)

    left_ref[...] = dot3(g_ref[...], v_ref[...])
    right_ref[...] = dot3(g_ref[...], next_ref[...], flip=True)

    from_below.wait_recv()
    y_ref[...] = dot3(v_ref[...], g_below[...])
    d2_ref[...] = pivot_ref[...] - dot3(y_ref[...], v_ref[...], flip=True)
    ring_w.forward()
    from_above.wait_recv()
    z_ref[...] = dot3(next_ref[...].T, g_above[...])
    d2_ref[...] = d2_ref[...] - dot3(z_ref[...], next_ref[...])
    ring_d.forward()

    newton_start(d2_ref[...], x_ref, 3)
    ring_u.forward()

    v_from_below.wait_recv()
    v2_ref[...] = -dot3(y_ref[...], v_below[...])
    v_from_above.wait_recv()
    u2_ref[...] = -dot3(z_ref[...], v_above[...], flip=True)
    above_left[...] = dot3(g_above[own, :], next_ref[...])
    above_right[...] = dot3(g_above[own, :], v_above[...], flip=True)
    below_right[...] = dot3(g_below[own, :], v_ref[...], flip=True)
    ring_w.done()
    ring_d.done()
    ring_u.done()
    sender.sent()


def third_kernel(
    parts, d2_ref, g2_ref, v2_ref, u2_ref, g_ref, left_ref, right_ref,
    above_left, above_right, below_right, sd_ref, wd_ref, su_ref,
    s_out, next_out, pivot_out,
    left2, right2, x_ref, y_ref, down_out, up_out, down_in, up_in,
    xs_out, ys_out, yd_out, xs_in, ys_in, yd_in, send_sems, recv_sems,
):
    sender = Sender(parts, send_sems, recv_sems)
    part, row = sender.part, sender.row
    quarter = s_out.shape[0]
    own = pl.ds(pl.multiple_of(row * quarter, quarter), quarter)
    sender.greet((1, 0), (-1, 0), (2, 0), (-2, 0))
    left2[...] = dot3(g2_ref[...], v2_ref[...])
    down_out[...] = dot3(v2_ref[:, own].T, left2[...])
    from_above = sender.send(down_out, down_in, parts=-2)
    right2[...] = dot3(g2_ref[...], u2_ref[...])
    up_out[...] = dot3(u2_ref[:, own].T, right2[...])
    from_below = sender.send(up_out, up_in, parts=2)

    y_ref[...] = dot3(left2[...], wd_ref[...]) + dot3(right2[...], su_ref[...])
    ys_out[...] = -dot3(above_left[...], y_ref[...])
    ys = sender.send(ys_out, ys_in, parts=1)
    x_ref[...] = dot3(left2[...], sd_ref[...]) + dot3(right2[...], wd_ref[...], flip=True)
    x_ref[...] = g2_ref[...] + dot3(x_ref[...], left2[...], flip=True) + dot3(
        y_ref[...], right2[...], flip=True
    )
    xs_out[...] = dot3(above_left[...], x_ref[...]) - dot3(above_right[...], y_ref[...], flip=True)
    xs = sender.send(xs_out, xs_in, parts=1)
    yd_out[...] = dot3(below_right[...], x_ref[...])
    yd = sender.send(yd_out, yd_in, parts=-1)

    from_above.wait_recv()
    from_below.wait_recv()
    pivot_out[...] = d2_ref[own, :] - down_in[...] - up_in[...]
    xs.wait_recv()
    s_out[...] = g_ref[own, :] + dot3(xs_in[...], left_ref[...], flip=True)
    ys.wait_recv()
    yd.wait_recv()
    y = ys_in[...] + yd_in[...]
    s_out[...] = s_out[...] + dot3(y, right_ref[...], flip=True)
    next_out[...] = jnp.where(part == parts - 1, 0.0, -y)
    sender.sent()


def local(pivot_blocks, lower_blocks, top_diagonal, top_coupling):
    parts = lax.axis_size("tm")
    size = pivot_blocks.shape[1]
    quarter = lower_blocks.shape[2]
    whole = jax.ShapeDtypeStruct((size, size), f32)
    strip = jax.ShapeDtypeStruct((quarter, size), f32)
    whole_space = pltpu.VMEM((size, size), f32)
    strip_space = pltpu.VMEM((quarter, size), f32)

    def call(kernel, identity, operands, results, scratch, copies):
        return pl.pallas_call(
            functools.partial(kernel, parts),
            out_shape=tuple(results),
            in_specs=[VMEM] * len(operands),
            out_specs=(VMEM,) * len(results),
            scratch_shapes=list(scratch)
            + [pltpu.SemaphoreType.DMA((copies,)), pltpu.SemaphoreType.DMA((copies,))],
            compiler_params=pltpu.CompilerParams(
                collective_id=identity, has_side_effects=True, vmem_limit_bytes=LIMIT
            ),
        )(*operands)

    pivot = pivot_blocks[0]
    v, v_next, x, sdq, wdq, suq = call(
        first_kernel, 0,
        (pivot, lower_blocks[0], top_diagonal[0], top_coupling[0]),
        [whole, whole, whole, strip, strip, strip], [strip_space], 12,
    )
    g = finish(pivot, x)
    d2, x2, v2, u2, left, right, above_left, above_right, below_right, sd, wd, su = call(
        second_kernel, 1,
        (pivot, g, v, v_next, sdq, wdq, suq),
        [whole] * 6 + [strip] * 3 + [whole] * 3, [whole_space] * 6, 16,
    )
    g2 = finish(d2, x2)
    s, coupling, reduced = call(
        third_kernel, 2,
        (d2, g2, v2, u2, g, left, right, above_left, above_right, below_right, sd, wd, su),
        [strip] * 3, [whole_space] * 4 + [strip_space] * 10, 5,
    )
    return (s[None], coupling[None], reduced[None])


def solution(mesh):
    placed = (
        P("tm", None, None),
        P("tm", None, "rows"),
        P("tm", "rows", None),
        P("tm", "rows", None),
    )
    return jax.shard_map(
        local,
        mesh=mesh,
        in_specs=placed,
        out_specs=(P("tm", "rows", None), P("tm", "rows", None), P("tm", "rows", None)),
        check_vma=False,
    )
```

time: 641 us -> 118 us (0.18); the launches traced: 628 us -> 116 us
  other arithmetic: 259 us -> 0 us
  waiting for transfers between devices: 203 us -> 0 us
  Pallas kernels: 0 us -> 112 us
  matrix products: 71 us -> 0 us
  starting transfers between devices: 38.6 us -> 0 us
  local copies, waits for them, and re-layouts: 36.9 us -> 3.46 us
  between operations: 20.3 us -> 0.67 us
    another operation x43 -> x0, other arithmetic: 249 us -> none  [the longest x29 163 us: local(): factor = jnp.linalg.cholesky(whole_pivot)]
    all_gather x7 -> x0, waiting for transfers between devices: 148 us -> none  [the longest x2 50.4 us: local(): lax.all_gather(left_columns, 'rows', axis=1, tiled=True)]
    pallas_call x0 -> x5, Pallas kernels: none -> 112 us  [the longest x3 104 us: call(): pl.pallas_call(functools.partial(kernel, parts), out_shape=tuple(results)...]
    ppermute x9 -> x0, waiting for transfers between devices: 54.2 us -> none  [passed_along(): lax.ppermute(value, axis, [(source, source + steps) for source in range(l...]
    dot_general x20 -> x0, matrix products: 47.2 us -> none  [the longest x8 21.5 us: product_over(): lax.dot_general(left, right, (((0,), (0,)), ((), ())), precision=precise,...]
    ppermute x9 -> x0, starting transfers between devices: 33.1 us -> none  [passed_along(): lax.ppermute(value, axis, [(source, source + steps) for source in range(l...]
    another operation x35 -> x0, local copies, waits for them, and re-layouts: 24 us -> none  [the longest x27 23.1 us: solve_with(): return jax.scipy.linalg.cho_solve((factor, True), right_side)]
    another operation x40 -> x0, matrix products: 23.8 us -> none  [the longest x28 14.7 us: solve_with(): return jax.scipy.linalg.cho_solve((factor, True), right_side)]
  transfers between devices with their start and end apart: 17 -> 0, of which waited for: 11 -> 0; matrix products, arithmetic and copies ran while one was open for 53% -> 0% of each run, Pallas kernels for 0% -> 0%
where the time goes in v1:
time: 118 us; the launch traced here: 116 us
  Pallas kernels  112 us (95%)
  local copies, waits for them, and re-layouts  3.46 us (3%)
    pallas_call x3, Pallas kernels, call(): pl.pallas_call(functools.partial(kernel, parts), out_shape=tuple(results)...  104 us
    pallas_call x2, Pallas kernels, finish(): pl.pallas_call(finish_kernel, out_shape=jax.ShapeDtypeStruct((size, size)...  8.4 us
    unnamed x7, local copies, waits for them, and re-layouts  3.46 us

profile of v1, /device:TPU:1, one launch (start us, length us, event | category | flops | bytes accessed | tf_op | source)
XLA Modules:
  0.0 116.1 jit_solution(473736640128592637)
XLA Ops:
  0.6 32.1 %shard_map.67 = (f32[512,512]{1,0:T(8,128)}, f32[512,512]{1,0:T(8,128)}, f32[512,512]{1,0:T(8,128)}, f32[128,512]{1,0:T(8,128)}, f32[128,512]{1,0:T(8,128)}, /*index=5*/f32[128,512]{1,0:T(8,128)}) custom-call(f32[512,512]{1,0:T(8,128)} %bitcast.7, f32[512,128]{1,0:T(8,128)} %bitcast.10, f32[128,512]{1,0:T(8,128)} %bitcast.11, f32[128,512]{1,0:T(8,128)} %bitcast.12), custom_call_target="tpu_custom_call" | custom-call | tf_op jit(solution)/shard_map/pallas_call | solution.py:338
  32.7 4.2 %shard_map.68.g_ref = f32[512,512]{1,0:T(8,128)} custom-call(f32[512,512]{1,0:T(8,128)} %bitcast.8, f32[512,512]{1,0:T(8,128)} %get-tuple-element.24.x_ref), custom_call_target="tpu_custom_call" | custom-call | tf_op jit(solution)/shard_map/pallas_call | solution.py:108
  36.9 38.1 %shard_map.69 = (f32[512,512]{1,0:T(8,128)}, f32[512,512]{1,0:T(8,128)}, f32[512,512]{1,0:T(8,128)}, f32[512,512]{1,0:T(8,128)}, f32[512,512]{1,0:T(8,128)}, /*i...) custom-call(f32[512,512]{1,0:T(8,128)} %bitcast.9, ...), custom_call_target="tpu_custom_call" | custom-call | tf_op jit(solution)/shard_map/pallas_call | solution.py:338
  75.1 4.2 %shard_map.70.g2_ref = f32[512,512]{1,0:T(8,128)} custom-call(f32[512,512]{1,0:T(8,128)} %get-tuple-element.30.pivot_ref.d2_ref, f32[512,512]{1,0:T(8,128)} %get-tuple-element.31.x_ref), custom_call_target="tpu_custom_call" | custom-call | tf_op jit(solution)/shard_map/pallas_call | solution.py:108
  79.3 33.3 %shard_map.71 = (f32[128,512]{1,0:T(8,128)}, f32[128,512]{1,0:T(8,128)}, f32[128,512]{1,0:T(8,128)}) custom-call(f32[512,512]{1,0:T(8,128)} %get-tuple-element.30.pivot_ref.d2_ref, f32[512,512]{1,0:T(8,128)} %shard_map.70.g2_ref, f32[512,512]{1,0:T(8,128)} %get-tuple-element.32.v2_ref, f32[512,512]{1,0:T(8,128)} %get-tuple-element.33.u2_ref, ...), custom_call_target="tpu_custom_call" | custom-call | tf_op jit(solution)/shard_map/pallas_call | solution.py:338
  112.6 0.0 copy-start.1
  112.6 1.7 %copy.10 = f32[1,128,512]{2,1,0:T(8,128)} copy(f32[1,128,512]{2,1,0:T(8,128)} %bitcast.15) | data formatting | bytes 524288
  114.3 0.0 copy-done.1
  114.3 0.0 copy-start
  114.3 0.7 copy.11
  115.0 0.3 copy-done
  115.4 0.7 copy.12
Async XLA Ops:
  112.6 1.7 %copy-start.1 = (f32[128,512]{1,0:T(8,128)S(1)}, f32[128,512]{1,0:T(8,128)}, u32[]{:S(2)}) copy-start(f32[128,512]{1,0:T(8,128)} %get-tuple-element.43) | copy-start | bytes 786436
  114.3 1.0 copy-start

commit v2 on v1

v2 whole, which is shorter than its diff:
```python
import functools

import jax
import jax.numpy as jnp
from jax import lax
from jax.experimental import pallas as pl
from jax.experimental.pallas import tpu as pltpu
from jax.sharding import PartitionSpec as P

f32 = jnp.float32
bf16 = jnp.bfloat16
MESH = pl.DeviceIdType.MESH
VMEM = pl.BlockSpec(memory_space=pltpu.VMEM)
LIMIT = 36 * 2**20


def dot(a, b, flip=False, precision=None):
    dims = (((1,), (1 if flip else 0,)), ((), ()))
    return lax.dot_general(a, b, dims, precision=precision, preferred_element_type=f32)


def split(x):
    high = x.astype(bf16)
    return high, (x - high.astype(f32)).astype(bf16)


def dot3(a, b, flip=False):
    ah, al = split(a)
    bh, bl = split(b)
    return dot(ah, bh, flip) + (dot(ah, bl, flip) + dot(al, bh, flip))


def dot1(a, b):
    return dot(a.astype(bf16), b.astype(bf16))


def full_dot(a, b):
    return dot(a, b, precision=lax.Precision.HIGHEST)


def eye(size):
    rows = lax.broadcasted_iota(jnp.int32, (size, size), 0)
    columns = lax.broadcasted_iota(jnp.int32, (size, size), 1)
    return rows == columns


def scales(pivot):
    only = jnp.where(eye(pivot.shape[0]), pivot, 0.0)
    return (
        lax.rsqrt(jnp.sum(only, axis=1, keepdims=True)),
        lax.rsqrt(jnp.sum(only, axis=0, keepdims=True)),
    )


def row_norm(x):
    return jnp.max(jnp.sum(jnp.abs(x), axis=1, keepdims=True), axis=0, keepdims=True)


def newton_start(scaled, steps):
    factor = jnp.minimum(1.0, 1.9 / row_norm(scaled))
    one = jnp.where(eye(scaled.shape[0]), 1.0, 0.0)
    rest = one - factor * scaled
    x = factor * (one + rest)
    for _ in range(steps):
        rest = dot1(rest, rest)
        x = x + dot1(x, rest)
    return x


def newton_end(x, out_ref, a_ref):
    size = a_ref.shape[0]

    def one():
        return jnp.where(eye(size), 1.0, 0.0)

    rest = one() - dot3(a_ref[...], x)
    first = row_norm(rest)[0, 0]
    out_ref[...] = x + dot1(x, rest)

    @pl.when(jnp.logical_not(first < 2.0**-7))
    def _():
        @pl.when(jnp.logical_not(first < 0.5))
        def _():
            out_ref[...] = one() / row_norm(a_ref[...])

        def more(state):
            count, norm = state
            return jnp.logical_and(count < 60, jnp.logical_not(norm < 1e-3))

        def step(state):
            count, _ = state
            rest = one() - full_dot(a_ref[...], out_ref[...])
            out_ref[...] = out_ref[...] + full_dot(out_ref[...], rest)
            return count + 1, row_norm(rest)[0, 0]

        lax.while_loop(more, step, (0, jnp.float32(1.0)))


def inverse_kernel(pivot_ref, out_ref, a_ref):
    column, row = scales(pivot_ref[...])
    a_ref[...] = pivot_ref[...] * column * row
    newton_end(newton_start(a_ref[...], 2), out_ref, a_ref)
    out_ref[...] = out_ref[...] * column * row


def finish_kernel(pivot_ref, x_ref, out_ref, a_ref):
    column, row = scales(pivot_ref[...])
    a_ref[...] = pivot_ref[...] * column * row
    newton_end(x_ref[...], out_ref, a_ref)
    out_ref[...] = out_ref[...] * column * row


def inverse(kernel, *operands):
    size = operands[0].shape[0]
    return pl.pallas_call(
        kernel,
        out_shape=jax.ShapeDtypeStruct((size, size), f32),
        in_specs=[VMEM] * len(operands),
        out_specs=VMEM,
        scratch_shapes=[pltpu.VMEM((size, size), f32)],
        compiler_params=pltpu.CompilerParams(vmem_limit_bytes=LIMIT),
    )(*operands)


class Sender:
    def __init__(self, parts, send_sems, recv_sems):
        self.parts, self.send_sems, self.recv_sems = parts, send_sems, recv_sems
        self.count = 0
        self.part = lax.axis_index("tm")
        self.row = lax.axis_index("rows")
        self.copies = []

    def device(self, parts=0, rows=0):
        return (
            lax.rem(self.part + (parts + self.parts), self.parts),
            lax.rem(self.row + (rows + 4), 4),
        )

    def greet(self, *offsets):
        barrier = pltpu.get_barrier_semaphore()
        for parts, rows in offsets:
            pl.semaphore_signal(barrier, inc=1, device_id=self.device(parts, rows), device_id_type=MESH)
        pl.semaphore_wait(barrier, len(offsets))

    def plan(self, source, target, parts=0, rows=0):
        copy = pltpu.make_async_remote_copy(
            src_ref=source,
            dst_ref=target,
            send_sem=self.send_sems.at[self.count],
            recv_sem=self.recv_sems.at[self.count],
            device_id=self.device(parts, rows),
            device_id_type=MESH,
        )
        self.count += 1
        return copy

    def send(self, source, target, parts=0, rows=0):
        copy = self.plan(source, target, parts, rows)
        copy.start()
        self.copies.append(copy)
        return copy

    def sent(self):
        for copy in self.copies:
            copy.wait_send()


class Ring:
    def __init__(self, sender, view):
        row = sender.row
        left, right = lax.rem(row + 3, 4), lax.rem(row + 1, 4)
        self.first = sender.plan(view(row), view(row), rows=1)
        self.second = sender.plan(view(row), view(row), rows=-1)
        self.third = sender.plan(view(left, 0), view(left, 0), rows=1)
        self.fourth = sender.plan(view(right, 1), view(right, 1), rows=-1)

    def start(self):
        self.first.start()
        self.second.start()

    def forward(self):
        self.first.wait_recv()
        self.third.start()
        self.second.wait_recv()
        self.fourth.start()

    def done(self):
        self.third.wait_recv()
        self.fourth.wait_recv()

    def sent(self):
        for copy in (self.first, self.second, self.third, self.fourth):
            copy.wait_send()


def upper(ref, i):
    step = ref.shape[0] // 4
    return ref.at[pl.ds(i * step, step), pl.ds(i * step, (4 - i) * step)]


def mirror(ref):
    step = ref.shape[0] // 4
    for i in range(4):
        for j in range(i + 1, 4):
            here, there = pl.ds(i * step, step), pl.ds(j * step, step)
            ref[there, here] = ref[here, there].T


def columns_of(ref):
    quarter = ref.shape[1] // 4
    half = ref.shape[0] // 2

    def view(q, h=None):
        rows = slice(None) if h is None else pl.ds(h * half, half)
        return ref.at[rows, pl.ds(pl.multiple_of(q * quarter, quarter), quarter)]

    return view


def rows_of(ref):
    quarter = ref.shape[0] // 4
    half = quarter // 2

    def view(q, h=None):
        if h is None:
            return ref.at[pl.ds(pl.multiple_of(q * quarter, quarter), quarter), :]
        return ref.at[pl.ds(pl.multiple_of(q * quarter + h * half, half), half), :]

    return view


def second_kernel(
    parts, pivot_ref, lower_ref, s_ref, w_ref, g_ref,
    d2_ref, x_ref, v2_ref, u2_ref, left_ref, right_ref, above_left, above_right, below_right,
    wd_ref, su_ref, sdq_ref,
    v_ref, next_ref, w_masked, g_below, g_above, v_below, v_above, z_ref, y_ref,
    send_sems, recv_sems,
):
    sender = Sender(parts, send_sems, recv_sems)
    part, row = sender.part, sender.row
    odd = lax.rem(part, 2) == 1
    even = lax.rem(part, 2) == 0
    quarter = lower_ref.shape[1]
    own = pl.ds(pl.multiple_of(row * quarter, quarter), quarter)
    left, right, far = (lax.rem(row + i, 4) for i in (3, 1, 2))
    v_ref[:, own] = jnp.where(part == 0, 0.0, lower_ref[...])
    w_masked[...] = jnp.where(part + 4 >= parts, 0.0, w_ref[...])
    view, target = columns_of(v_ref), columns_of(next_ref)
    sender.greet((0, 1), (0, -1), (1, 0), (-1, 0), (2, 0), (-2, 0))

    next_own = sender.send(view(row), target(row), parts=-1)
    ring_v = Ring(sender, view)
    ring_v.start()
    w_own = sender.send(w_masked, rows_of(wd_ref)(row), parts=2)
    from_below = [sender.send(upper(g_ref, i), upper(g_below, i), parts=1) for i in range(4)]
    from_above = [sender.send(upper(g_ref, i), upper(g_above, i), parts=-1) for i in range(4)]
    su_own = sender.send(s_ref, rows_of(su_ref)(row), parts=-2)
    ring_next = Ring(sender, target)
    passed = [
        sender.plan(view(q, h), target(q, h), parts=-1)
        for q, h in ((left, None), (right, None), (far, 0), (far, 1))
    ]

    next_own.wait_recv()

    @pl.when(odd)
    def _():
        ring_next.start()

    ring_v.forward()

    @pl.when(odd)
    def _():
        passed[0].start()
        passed[1].start()

    w_own.wait_recv()
    ring_w = Ring(sender, rows_of(wd_ref))
    ring_w.start()

    @pl.when(odd)
    def _():
        ring_next.forward()

    ring_v.done()

    @pl.when(odd)
    def _():
        passed[2].start()
        passed[3].start()

    v_from_below = sender.send(v_ref, v_below, parts=1)
    sd_own = sender.send(s_ref, sdq_ref, parts=2)
    left_ref[...] = dot3(g_ref[...], v_ref[...])

    @pl.when(odd)
    def _():
        ring_next.done()

    @pl.when(even)
    def _():
        for copy in passed:
            copy.wait_recv()

    v_from_above = sender.send(next_ref, v_above, parts=-1)

    for copy in from_below:
        copy.wait_recv()
    mirror(g_below)
    y_ref[...] = dot3(v_ref[...], g_below[...])
    d2_ref[...] = pivot_ref[...] - dot3(y_ref[...], v_ref[...], flip=True)
    su_own.wait_recv()
    ring_u = Ring(sender, rows_of(su_ref))
    ring_u.start()
    for copy in from_above:
        copy.wait_recv()
    mirror(g_above)
    z_ref[...] = dot3(next_ref[...].T, g_above[...])
    d2_ref[...] = d2_ref[...] - dot3(z_ref[...], next_ref[...])
    ring_w.forward()

    column, line = scales(d2_ref[...])
    x_ref[...] = newton_start(d2_ref[...] * column * line, 3)
    right_ref[...] = dot3(g_ref[...], next_ref[...], flip=True)
    above_left[...] = dot3(g_above[own, :], next_ref[...])
    below_right[...] = dot3(g_below[own, :], v_ref[...], flip=True)
    ring_u.forward()

    v_from_above.wait_recv()
    u2_ref[...] = -dot3(z_ref[...], v_above[...], flip=True)
    above_right[...] = dot3(g_above[own, :], v_above[...], flip=True)
    v_from_below.wait_recv()
    v2_ref[...] = -dot3(y_ref[...], v_below[...])
    sd_own.wait_recv()
    ring_w.done()
    ring_u.done()
    sender.sent()
    for ring in (ring_v, ring_w, ring_u):
        ring.sent()

    @pl.when(odd)
    def _():
        ring_next.sent()
        for copy in passed:
            copy.wait_send()


def third_kernel(
    parts, g2_ref, v2_ref, u2_ref, left_ref, right_ref,
    above_left, above_right, below_right, wd_ref, su_ref, sdq_ref,
    s_out, y_out, down_in, up_in,
    sd_ref, left2, right2, x_ref, y_ref, down_out, up_out,
    xs_out, ys_out, yd_out, xs_in, ys_in, yd_in, send_sems, recv_sems,
):
    sender = Sender(parts, send_sems, recv_sems)
    row = sender.row
    quarter = s_out.shape[0]
    own = pl.ds(pl.multiple_of(row * quarter, quarter), quarter)
    sd_ref[own, :] = sdq_ref[...]
    sender.greet((0, 1), (0, -1), (1, 0), (-1, 0), (2, 0), (-2, 0))
    ring_d = Ring(sender, rows_of(sd_ref))
    ring_d.start()
    left2[...] = dot3(g2_ref[...], v2_ref[...])
    right2[...] = dot3(g2_ref[...], u2_ref[...])
    y_ref[...] = dot3(left2[...], wd_ref[...]) + dot3(right2[...], su_ref[...])
    ys_out[...] = -dot3(above_left[...], y_ref[...])
    ys = sender.send(ys_out, ys_in, parts=1)
    ring_d.forward()
    down_out[...] = dot3(v2_ref[:, own].T, left2[...])
    from_above = sender.send(down_out, down_in, parts=-2)
    up_out[...] = dot3(u2_ref[:, own].T, right2[...])
    from_below = sender.send(up_out, up_in, parts=2)
    x_ref[...] = dot3(right2[...], wd_ref[...], flip=True)
    ring_d.done()
    x_ref[...] = x_ref[...] + dot3(left2[...], sd_ref[...])
    x_ref[...] = g2_ref[...] + dot3(x_ref[...], left2[...], flip=True) + dot3(
        y_ref[...], right2[...], flip=True
    )
    xs_out[...] = dot3(above_left[...], x_ref[...]) - dot3(above_right[...], y_ref[...], flip=True)
    xs = sender.send(xs_out, xs_in, parts=1)
    yd_out[...] = dot3(below_right[...], x_ref[...])
    yd = sender.send(yd_out, yd_in, parts=-1)

    from_above.wait_recv()
    from_below.wait_recv()
    ys.wait_recv()
    yd.wait_recv()
    y_out[...] = ys_in[...] + yd_in[...]
    s_out[...] = dot3(y_out[...], right_ref[...], flip=True)
    xs.wait_recv()
    s_out[...] = s_out[...] + dot3(xs_in[...], left_ref[...], flip=True)
    sender.sent()
    ring_d.sent()


def local(pivot_blocks, lower_blocks, top_diagonal, top_coupling):
    parts = lax.axis_size("tm")
    size = pivot_blocks.shape[1]
    quarter = lower_blocks.shape[2]
    whole = jax.ShapeDtypeStruct((size, size), f32)
    strip = jax.ShapeDtypeStruct((quarter, size), f32)
    whole_space = pltpu.VMEM((size, size), f32)
    strip_space = pltpu.VMEM((quarter, size), f32)

    def call(kernel, identity, operands, results, scratch, copies):
        return pl.pallas_call(
            functools.partial(kernel, parts),
            out_shape=tuple(results),
            in_specs=[VMEM] * len(operands),
            out_specs=(VMEM,) * len(results),
            scratch_shapes=list(scratch)
            + [pltpu.SemaphoreType.DMA((copies,)), pltpu.SemaphoreType.DMA((copies,))],
            compiler_params=pltpu.CompilerParams(
                collective_id=identity, has_side_effects=True, vmem_limit_bytes=LIMIT
            ),
        )(*operands)

    pivot = pivot_blocks[0]
    g = inverse(inverse_kernel, pivot)
    d2, x2, v2, u2, left, right, above_left, above_right, below_right, wd, su, sdq = call(
        second_kernel, 0,
        (pivot, lower_blocks[0], top_diagonal[0], top_coupling[0], g),
        [whole] * 6 + [strip] * 3 + [whole] * 2 + [strip],
        [whole_space] * 2 + [strip_space] + [whole_space] * 6, 34,
    )
    g2 = inverse(finish_kernel, d2, x2)
    s, y, down, up = call(
        third_kernel, 1,
        (g2, v2, u2, left, right, above_left, above_right, below_right, wd, su, sdq),
        [strip] * 4, [whole_space] * 5 + [strip_space] * 8, 9,
    )
    start = lax.axis_index("rows") * quarter
    s = lax.dynamic_slice_in_dim(g, start, quarter, 0) + s
    reduced = lax.dynamic_slice_in_dim(d2, start, quarter, 0) - down - up
    coupling = jnp.where(lax.axis_index("tm") == parts - 1, 0.0, -y)
    return (s[None], coupling[None], reduced[None])


def solution(mesh):
    placed = (
        P("tm", None, None),
        P("tm", None, "rows"),
        P("tm", "rows", None),
        P("tm", "rows", None),
    )
    return jax.shard_map(
        local,
        mesh=mesh,
        in_specs=placed,
        out_specs=(P("tm", "rows", None), P("tm", "rows", None), P("tm", "rows", None)),
        check_vma=False,
    )
```

time: 118 us -> 83.8 us (0.71); the launches traced: 116 us -> 83.6 us
  Pallas kernels: 112 us -> 80.1 us
  local copies, waits for them, and re-layouts: 3.46 us -> 1.23 us
  other arithmetic: 0 us -> 1.62 us
    pallas_call x3 -> x2, Pallas kernels: 104 us -> 75.1 us  [call(): pl.pallas_call(functools.partial(kernel, parts), out_shape=tuple(results)...]
    pallas_call x2, Pallas kernels: 8.4 us -> 4.96 us  [inverse(): pl.pallas_call(kernel, out_shape=jax.ShapeDtypeStruct((size, size), f32),...]
    unnamed x7 -> x8, local copies, waits for them, and re-layouts: 3.46 us -> 1.23 us
    broadcast_in_dim x0 -> x2, other arithmetic: none -> 1.62 us  [local(): return (s[None], coupling[None], reduced[None])]
where the time goes in v2:
time: 83.8 us; the launch traced here: 83.6 us
  Pallas kernels  80.1 us (96%)
  other arithmetic  1.62 us (2%)
  local copies, waits for them, and re-layouts  1.23 us (1%)
    pallas_call x2, Pallas kernels, call(): pl.pallas_call(functools.partial(kernel, parts), out_shape=tuple(results)...  75.1 us
    pallas_call x2, Pallas kernels, inverse(): pl.pallas_call(kernel, out_shape=jax.ShapeDtypeStruct((size, size), f32),...  4.96 us

profile of v2, /device:TPU:1, one launch (start us, length us, event | category | flops | bytes accessed | tf_op | source)
XLA Modules:
  0.0 83.6 jit_solution(1515303199364766379)
XLA Ops:
  0.6 0.0 copy-start
  0.6 1.2 %copy-done = f32[1,512,512]{2,1,0:T(8,128)S(1)} copy-done((f32[1,512,512]{2,1,0:T(8,128)S(1)}, f32[1,512,512]{2,1,0:T(8,128)}, u32[]{:S(2)}) %copy-start) | copy-done | bytes 1048600
  1.9 0.0 copy-start.1
  1.9 0.0 copy-start.2
  1.9 0.0 copy-start.3
  1.9 3.2 %shard_map.67.g_ref = f32[512,512]{1,0:T(8,128)S(1)} custom-call(f32[512,512]{1,0:T(8,128)S(1)} %bitcast.10), custom_call_target="tpu_custom_call" | custom-call | tf_op jit(solution)/shard_map/pallas_call | solution.py:115
  5.1 0.0 copy-done.1
  5.1 0.0 copy-done.2
  5.1 0.0 copy-done.3
  5.2 50.4 %shard_map.68 = (f32[512,512]{1,0:T(8,128)S(1)}, f32[512,512]{1,0:T(8,128)S(1)}, f32[512,512]{1,0:T(8,128)S(1)}, f32[512,512]{1,0:T(8,128)S(1)}, f32[512,512]{1,...) custom-call(f32[512,512]{1,0:T(8,128)S(1)} %bitcast.11, ...), custom_call_target="tpu_custom_call" | custom-call | tf_op jit(solution)/shard_map/pallas_call | solution.py:406
  55.6 1.7 %shard_map.69.g2_ref = f32[512,512]{1,0:T(8,128)S(1)} custom-call(f32[512,512]{1,0:T(8,128)S(1)} %get-tuple-element.19.pivot_ref, f32[512,512]{1,0:T(8,128)S(1)} %get-tuple-element.20.x_ref), custom_call_target="tpu_custom_call" | custom-call | tf_op jit(solution)/shard_map/pallas_call | solution.py:115
  57.3 24.7 %shard_map.70 = (f32[128,512]{1,0:T(8,128)S(1)}, f32[128,512]{1,0:T(8,128)S(1)}, f32[128,512]{1,0:T(8,128)S(1)}, f32[128,512]{1,0:T(8,128)S(1)}) custom-call(f32[512,512]{1,0:T(8,128)S(1)} %shard_map.69.g2_ref, f32[512,512]{1,0:T(8,128)S(1)} %get-tuple-element.21.v2_ref, f32[512,512]{1,0:T(8,128)S(1)} %get-tuple-element.22.u2_ref, ...), custom_call_target="tpu_custom_call" | custom-call | tf_op jit(solution)/shard_map/pallas_call | solution.py:406
  82.0 0.9 %subtract_bitcast_fusion = (f32[1,128,512]{2,1,0:T(8,128)}, f32[1,128,512]{2,1,0:T(8,128)}) fusion(f32[128,512]{1,0:T(8,128)S(1)} %get-tuple-element.34, f32[128,512]{1,0:T(8,128)S(1)} %get-tuple-element.33, f32[512,512]{1,0:T(8,128)S(1)} %get-tuple-element.19.pivot_ref, s32[]{:T(128)S(6)} %select_n.12, f32[128,512]{1,0:T(8,128)S(1)} %get-tuple-element.32, ...), kind=kLoop, calls=%fused_computation | loop fusion | flops 262144 | bytes 1572869 | tf_op jit(solution)/shard_map/broadcast_in_dim | solution.py:436
  82.9 0.7 add_bitcast_fusion
Async XLA Ops:
  0.6 1.2 %copy-start = (f32[1,512,512]{2,1,0:T(8,128)S(1)}, f32[1,512,512]{2,1,0:T(8,128)}, u32[]{:S(2)}) copy-start(f32[1,512,512]{2,1,0:T(8,128)} %param.4) | copy-start | bytes 3145732
  1.9 3.3 %copy-start.1 = (f32[1,512,128]{2,1,0:T(8,128)S(1)}, f32[1,512,128]{2,1,0:T(8,128)}, u32[]{:S(2)}) copy-start(f32[1,512,128]{2,1,0:T(8,128)} %param.5) | copy-start | bytes 786436
  1.9 3.3 %copy-start.2 = (f32[1,128,512]{2,1,0:T(8,128)S(1)}, f32[1,128,512]{2,1,0:T(8,128)}, u32[]{:S(2)}) copy-start(f32[1,128,512]{2,1,0:T(8,128)} %param.6) | copy-start | bytes 786436
  1.9 3.3 %copy-start.3 = (f32[1,128,512]{2,1,0:T(8,128)S(1)}, f32[1,128,512]{2,1,0:T(8,128)}, u32[]{:S(2)}) copy-start(f32[1,128,512]{2,1,0:T(8,128)} %param.7) | copy-start | bytes 786436

commit v3 on v2

--- a/solution.py
+++ b/solution.py
@@ -252,14 +252,15 @@
     ring_v = Ring(sender, view)
     ring_v.start()
     w_own = sender.send(w_masked, rows_of(wd_ref)(row), parts=2)
+    su_own = sender.send(s_ref, rows_of(su_ref)(row), parts=-2)
     from_below = [sender.send(upper(g_ref, i), upper(g_below, i), parts=1) for i in range(4)]
     from_above = [sender.send(upper(g_ref, i), upper(g_above, i), parts=-1) for i in range(4)]
-    su_own = sender.send(s_ref, rows_of(su_ref)(row), parts=-2)
     ring_next = Ring(sender, target)
     passed = [
         sender.plan(view(q, h), target(q, h), parts=-1)
         for q, h in ((left, None), (right, None), (far, 0), (far, 1))
     ]
+    v_from_above = sender.plan(next_ref, v_above, parts=-1)
 
     next_own.wait_recv()
 
@@ -277,6 +278,9 @@
     w_own.wait_recv()
     ring_w = Ring(sender, rows_of(wd_ref))
     ring_w.start()
+    su_own.wait_recv()
+    ring_u = Ring(sender, rows_of(su_ref))
+    ring_u.start()
 
     @pl.when(odd)
     def _():
@@ -293,48 +297,46 @@
     sd_own = sender.send(s_ref, sdq_ref, parts=2)
     left_ref[...] = dot3(g_ref[...], v_ref[...])
 
-    @pl.when(odd)
-    def _():
-        ring_next.done()
-
     @pl.when(even)
     def _():
         for copy in passed:
             copy.wait_recv()
-
-    v_from_above = sender.send(next_ref, v_above, parts=-1)
+        v_from_above.start()
 
     for copy in from_below:
         copy.wait_recv()
     mirror(g_below)
     y_ref[...] = dot3(v_ref[...], g_below[...])
     d2_ref[...] = pivot_ref[...] - dot3(y_ref[...], v_ref[...], flip=True)
-    su_own.wait_recv()
-    ring_u = Ring(sender, rows_of(su_ref))
-    ring_u.start()
+    ring_w.forward()
+    below_right[...] = dot3(g_below[own, :], v_ref[...], flip=True)
+
+    @pl.when(odd)
+    def _():
+        ring_next.done()
+        v_from_above.start()
+
     for copy in from_above:
         copy.wait_recv()
     mirror(g_above)
     z_ref[...] = dot3(next_ref[...].T, g_above[...])
     d2_ref[...] = d2_ref[...] - dot3(z_ref[...], next_ref[...])
-    ring_w.forward()
 
     column, line = scales(d2_ref[...])
     x_ref[...] = newton_start(d2_ref[...] * column * line, 3)
+    ring_u.forward()
     right_ref[...] = dot3(g_ref[...], next_ref[...], flip=True)
     above_left[...] = dot3(g_above[own, :], next_ref[...])
-    below_right[...] = dot3(g_below[own, :], v_ref[...], flip=True)
-    ring_u.forward()
-
+    v_from_below.wait_recv()
+    v2_ref[...] = -dot3(y_ref[...], v_below[...])
     v_from_above.wait_recv()
     u2_ref[...] = -dot3(z_ref[...], v_above[...], flip=True)
     above_right[...] = dot3(g_above[own, :], v_above[...], flip=True)
-    v_from_below.wait_recv()
-    v2_ref[...] = -dot3(y_ref[...], v_below[...])
     sd_own.wait_recv()
     ring_w.done()
     ring_u.done()
     sender.sent()
+    v_from_above.wait_send()
     for ring in (ring_v, ring_w, ring_u):
         ring.sent()
 
@@ -349,7 +351,7 @@
     parts, g2_ref, v2_ref, u2_ref, left_ref, right_ref,
     above_left, above_right, below_right, wd_ref, su_ref, sdq_ref,
     s_out, y_out, down_in, up_in,
-    sd_ref, left2, right2, x_ref, y_ref, down_out, up_out,
+    sd_ref, left2, c_ref, x_ref, y_ref, down_out, up_out,
     xs_out, ys_out, yd_out, xs_in, ys_in, yd_in, send_sems, recv_sems,
 ):
     sender = Sender(parts, send_sems, recv_sems)
@@ -360,22 +362,26 @@
     sender.greet((0, 1), (0, -1), (1, 0), (-1, 0), (2, 0), (-2, 0))
     ring_d = Ring(sender, rows_of(sd_ref))
     ring_d.start()
-    left2[...] = dot3(g2_ref[...], v2_ref[...])
-    right2[...] = dot3(g2_ref[...], u2_ref[...])
-    y_ref[...] = dot3(left2[...], wd_ref[...]) + dot3(right2[...], su_ref[...])
+    c_ref[...] = dot3(v2_ref[...], wd_ref[...]) + dot3(u2_ref[...], su_ref[...])
+    y_ref[...] = dot3(g2_ref[...], c_ref[...])
     ys_out[...] = -dot3(above_left[...], y_ref[...])
     ys = sender.send(ys_out, ys_in, parts=1)
-    ring_d.forward()
+    left2[...] = dot3(g2_ref[...], v2_ref[...])
     down_out[...] = dot3(v2_ref[:, own].T, left2[...])
     from_above = sender.send(down_out, down_in, parts=-2)
-    up_out[...] = dot3(u2_ref[:, own].T, right2[...])
+    x_ref[...] = dot3(g2_ref[...], u2_ref[...])
+    up_out[...] = dot3(u2_ref[:, own].T, x_ref[...])
     from_below = sender.send(up_out, up_in, parts=2)
-    x_ref[...] = dot3(right2[...], wd_ref[...], flip=True)
+    x_ref[...] = dot3(u2_ref[...], wd_ref[...], flip=True)
+    ring_d.forward()
+    x_ref[...] = dot3(x_ref[...], v2_ref[...], flip=True) + dot3(
+        c_ref[...], u2_ref[...], flip=True
+    )
+    c_ref[...] = dot3(g2_ref[...], x_ref[...])
+    x_ref[...] = g2_ref[...] + dot3(c_ref[...], g2_ref[...])
     ring_d.done()
-    x_ref[...] = x_ref[...] + dot3(left2[...], sd_ref[...])
-    x_ref[...] = g2_ref[...] + dot3(x_ref[...], left2[...], flip=True) + dot3(
-        y_ref[...], right2[...], flip=True
-    )
+    c_ref[...] = dot3(left2[...], sd_ref[...])
+    x_ref[...] = x_ref[...] + dot3(c_ref[...], left2[...], flip=True)
     xs_out[...] = dot3(above_left[...], x_ref[...]) - dot3(above_right[...], y_ref[...], flip=True)
     xs = sender.send(xs_out, xs_in, parts=1)
     yd_out[...] = dot3(below_right[...], x_ref[...])

time: 83.8 us -> 84.1 us (level)
  no operation moved by 1% of the time
where the time goes in v3:
time: 84.1 us; the launch traced here: 83.9 us
  Pallas kernels  80.3 us (95%)
  other arithmetic  1.62 us (2%)
  local copies, waits for them, and re-layouts  1.23 us (1%)
    pallas_call x2, Pallas kernels, call(): pl.pallas_call(functools.partial(kernel, parts), out_shape=tuple(results)...  75.4 us
    pallas_call x2, Pallas kernels, inverse(): pl.pallas_call(kernel, out_shape=jax.ShapeDtypeStruct((size, size), f32),...  4.96 us

profile of v3, /device:TPU:1, one launch (start us, length us, event | category | flops | bytes accessed | tf_op | source)
XLA Modules:
  0.0 83.9 jit_solution(16464706214713478307)
XLA Ops:
  0.6 0.0 copy-start
  0.6 1.2 %copy-done = f32[1,512,512]{2,1,0:T(8,128)S(1)} copy-done((f32[1,512,512]{2,1,0:T(8,128)S(1)}, f32[1,512,512]{2,1,0:T(8,128)}, u32[]{:S(2)}) %copy-start) | copy-done | bytes 1048600
  1.9 0.0 copy-start.1
  1.9 0.0 copy-start.2
  1.9 0.0 copy-start.3
  1.9 3.2 %shard_map.67.g_ref = f32[512,512]{1,0:T(8,128)S(1)} custom-call(f32[512,512]{1,0:T(8,128)S(1)} %bitcast.10), custom_call_target="tpu_custom_call" | custom-call | tf_op jit(solution)/shard_map/pallas_call | solution.py:115
  5.1 0.0 copy-done.1
  5.1 0.0 copy-done.2
  5.1 0.0 copy-done.3
  5.2 52.4 %shard_map.68 = (f32[512,512]{1,0:T(8,128)S(1)}, f32[512,512]{1,0:T(8,128)S(1)}, f32[512,512]{1,0:T(8,128)S(1)}, f32[512,512]{1,0:T(8,128)S(1)}, f32[512,512]{1,...) custom-call(f32[512,512]{1,0:T(8,128)S(1)} %bitcast.11, ...), custom_call_target="tpu_custom_call" | custom-call | tf_op jit(solution)/shard_map/pallas_call | solution.py:412
  57.6 1.7 %shard_map.69.g2_ref = f32[512,512]{1,0:T(8,128)S(1)} custom-call(f32[512,512]{1,0:T(8,128)S(1)} %get-tuple-element.19.pivot_ref, f32[512,512]{1,0:T(8,128)S(1)} %get-tuple-element.20.x_ref), custom_call_target="tpu_custom_call" | custom-call | tf_op jit(solution)/shard_map/pallas_call | solution.py:115
  59.3 23.0 %shard_map.70 = (f32[128,512]{1,0:T(8,128)S(1)}, f32[128,512]{1,0:T(8,128)S(1)}, f32[128,512]{1,0:T(8,128)S(1)}, f32[128,512]{1,0:T(8,128)S(1)}) custom-call(f32[512,512]{1,0:T(8,128)S(1)} %shard_map.69.g2_ref, f32[512,512]{1,0:T(8,128)S(1)} %get-tuple-element.21.v2_ref, f32[512,512]{1,0:T(8,128)S(1)} %get-tuple-element.22.u2_ref, ...), custom_call_target="tpu_custom_call" | custom-call | tf_op jit(solution)/shard_map/pallas_call | solution.py:412
  82.3 0.9 %subtract_bitcast_fusion = (f32[1,128,512]{2,1,0:T(8,128)}, f32[1,128,512]{2,1,0:T(8,128)}) fusion(f32[128,512]{1,0:T(8,128)S(1)} %get-tuple-element.34, f32[128,512]{1,0:T(8,128)S(1)} %get-tuple-element.33, f32[512,512]{1,0:T(8,128)S(1)} %get-tuple-element.19.pivot_ref, s32[]{:T(128)S(6)} %select_n.12, f32[128,512]{1,0:T(8,128)S(1)} %get-tuple-element.32, ...), kind=kLoop, calls=%fused_computation | loop fusion | flops 262144 | bytes 1572869 | tf_op jit(solution)/shard_map/broadcast_in_dim | solution.py:442
  83.2 0.7 add_bitcast_fusion
Async XLA Ops:
  0.6 1.2 %copy-start = (f32[1,512,512]{2,1,0:T(8,128)S(1)}, f32[1,512,512]{2,1,0:T(8,128)}, u32[]{:S(2)}) copy-start(f32[1,512,512]{2,1,0:T(8,128)} %param.4) | copy-start | bytes 3145732
  1.9 3.3 %copy-start.1 = (f32[1,512,128]{2,1,0:T(8,128)S(1)}, f32[1,512,128]{2,1,0:T(8,128)}, u32[]{:S(2)}) copy-start(f32[1,512,128]{2,1,0:T(8,128)} %param.5) | copy-start | bytes 786436
  1.9 3.3 %copy-start.2 = (f32[1,128,512]{2,1,0:T(8,128)S(1)}, f32[1,128,512]{2,1,0:T(8,128)}, u32[]{:S(2)}) copy-start(f32[1,128,512]{2,1,0:T(8,128)} %param.6) | copy-start | bytes 786436
  1.9 3.3 %copy-start.3 = (f32[1,128,512]{2,1,0:T(8,128)S(1)}, f32[1,128,512]{2,1,0:T(8,128)}, u32[]{:S(2)}) copy-start(f32[1,128,512]{2,1,0:T(8,128)} %param.7) | copy-start | bytes 786436

commit v4 on v3

--- a/solution.py
+++ b/solution.py
@@ -56,67 +56,84 @@
     return jnp.max(jnp.sum(jnp.abs(x), axis=1, keepdims=True), axis=0, keepdims=True)
 
 
-def newton_start(scaled, steps):
+def steer(scaled):
     factor = jnp.minimum(1.0, 1.9 / row_norm(scaled))
-    one = jnp.where(eye(scaled.shape[0]), 1.0, 0.0)
-    rest = one - factor * scaled
-    x = factor * (one + rest)
+    rest = jnp.where(eye(scaled.shape[0]), 1.0, 0.0) - factor * scaled
+    return factor, rest, row_norm(rest)
+
+
+def newton(x, rest, steps):
     for _ in range(steps):
         rest = dot1(rest, rest)
         x = x + dot1(x, rest)
     return x
 
 
-def newton_end(x, out_ref, a_ref):
-    size = a_ref.shape[0]
-
-    def one():
-        return jnp.where(eye(size), 1.0, 0.0)
-
-    rest = one() - dot3(a_ref[...], x)
-    first = row_norm(rest)[0, 0]
-    out_ref[...] = x + dot1(x, rest)
-
-    @pl.when(jnp.logical_not(first < 2.0**-7))
-    def _():
-        @pl.when(jnp.logical_not(first < 0.5))
-        def _():
-            out_ref[...] = one() / row_norm(a_ref[...])
-
-        def more(state):
-            count, norm = state
-            return jnp.logical_and(count < 60, jnp.logical_not(norm < 1e-3))
-
-        def step(state):
-            count, _ = state
-            rest = one() - full_dot(a_ref[...], out_ref[...])
-            out_ref[...] = out_ref[...] + full_dot(out_ref[...], rest)
-            return count + 1, row_norm(rest)[0, 0]
-
-        lax.while_loop(more, step, (0, jnp.float32(1.0)))
-
-
-def inverse_kernel(pivot_ref, out_ref, a_ref):
+def newton_start(scaled, steps):
+    factor, rest, _ = steer(scaled)
+    one = jnp.where(eye(scaled.shape[0]), 1.0, 0.0)
+    return newton(factor * (one + rest), rest, steps)
+
+
+def settle(out_ref, a_ref):
+    def more(state):
+        count, norm = state
+        return jnp.logical_and(count < 60, jnp.logical_not(norm < 1e-3))
+
+    def step(state):
+        count, _ = state
+        one = jnp.where(eye(a_ref.shape[0]), 1.0, 0.0)
+        rest = one - full_dot(a_ref[...], out_ref[...])
+        out_ref[...] = out_ref[...] + full_dot(out_ref[...], rest)
+        return count + 1, row_norm(rest)[0, 0]
+
+    lax.while_loop(more, step, (0, jnp.float32(1.0)))
+
+
+def begin_kernel(pivot_ref, x_ref, rest_ref, flag_ref, a_ref):
     column, row = scales(pivot_ref[...])
     a_ref[...] = pivot_ref[...] * column * row
-    newton_end(newton_start(a_ref[...], 2), out_ref, a_ref)
-    out_ref[...] = out_ref[...] * column * row
+    one = jnp.where(eye(a_ref.shape[0]), 1.0, 0.0)
+    factor, rest, norm = steer(a_ref[...])
+    x_ref[...] = factor * (one + rest)
+    rest_ref[...] = rest
+    flag_ref[...] = jnp.ones_like(flag_ref)
+
+    @pl.when(jnp.logical_not(norm[0, 0] < 0.7))
+    def _():
+        x_ref[...] = jnp.where(eye(a_ref.shape[0]), 1.0, 0.0) / row_norm(a_ref[...])
+        settle(x_ref, a_ref)
+        rest_ref[...] = jnp.zeros_like(rest_ref)
+        flag_ref[...] = jnp.zeros_like(flag_ref)
 
 
 def finish_kernel(pivot_ref, x_ref, out_ref, a_ref):
     column, row = scales(pivot_ref[...])
     a_ref[...] = pivot_ref[...] * column * row
-    newton_end(x_ref[...], out_ref, a_ref)
+    one = jnp.where(eye(a_ref.shape[0]), 1.0, 0.0)
+    x = x_ref[...]
+    rest = one - dot3(a_ref[...], x)
+    first = row_norm(rest)[0, 0]
+    out_ref[...] = x + dot1(x, rest)
+
+    @pl.when(jnp.logical_not(first < 2.0**-7))
+    def _():
+        @pl.when(jnp.logical_not(first < 0.5))
+        def _():
+            out_ref[...] = jnp.where(eye(a_ref.shape[0]), 1.0, 0.0) / row_norm(a_ref[...])
+
+        settle(out_ref, a_ref)
+
     out_ref[...] = out_ref[...] * column * row
 
 
-def inverse(kernel, *operands):
+def alone(kernel, results, *operands):
     size = operands[0].shape[0]
     return pl.pallas_call(
         kernel,
-        out_shape=jax.ShapeDtypeStruct((size, size), f32),
+        out_shape=results,
         in_specs=[VMEM] * len(operands),
-        out_specs=VMEM,
+        out_specs=jax.tree.map(lambda _: VMEM, results),
         scratch_shapes=[pltpu.VMEM((size, size), f32)],
         compiler_params=pltpu.CompilerParams(vmem_limit_bytes=LIMIT),
     )(*operands)
@@ -229,11 +246,34 @@
     return view
 
 
+def blocks_of(ref):
+    half = ref.shape[2] // 2
+
+    def view(q, h=None):
+        if h is None:
+            return ref.at[q]
+        return ref.at[q, :, pl.ds(h * half, half), :]
+
+    return view
+
+
+def unpack(ref, blocks_ref):
+    step = ref.shape[0] // 4
+
+    def place(q):
+        return pl.ds(q % 4 * step, step)
+
+    for q in range(4):
+        for k in range(3):
+            ref[place(q), place(q + k)] = blocks_ref[q, k]
+        ref[place(q + 1), place(q)] = blocks_ref[q, 1].T
+
+
 def second_kernel(
-    parts, pivot_ref, lower_ref, s_ref, w_ref, g_ref,
-    d2_ref, x_ref, v2_ref, u2_ref, left_ref, right_ref, above_left, above_right, below_right,
+    parts, pivot_ref, lower_ref, s_ref, w_ref, start_ref, rest_ref, flag_ref,
+    g_ref, d2_ref, x_ref, v2_ref, u2_ref, left_ref, right_ref, above_left, above_right, below_right,
     wd_ref, su_ref, sdq_ref,
-    v_ref, next_ref, w_masked, g_below, g_above, v_below, v_above, z_ref, y_ref,
+    v_ref, next_ref, w_masked, s_packed, su_blocks, g_below, g_above, v_below, v_above, z_ref, y_ref,
     send_sems, recv_sems,
 ):
     sender = Sender(parts, send_sems, recv_sems)
@@ -245,6 +285,9 @@
     left, right, far = (lax.rem(row + i, 4) for i in (3, 1, 2))
     v_ref[:, own] = jnp.where(part == 0, 0.0, lower_ref[...])
     w_masked[...] = jnp.where(part + 4 >= parts, 0.0, w_ref[...])
+    for k in range(3):
+        column = pl.multiple_of(lax.rem(row + k, 4) * quarter, quarter)
+        s_packed[k] = s_ref[:, pl.ds(column, quarter)]
     view, target = columns_of(v_ref), columns_of(next_ref)
     sender.greet((0, 1), (0, -1), (1, 0), (-1, 0), (2, 0), (-2, 0))
 
@@ -252,7 +295,14 @@
     ring_v = Ring(sender, view)
     ring_v.start()
     w_own = sender.send(w_masked, rows_of(wd_ref)(row), parts=2)
-    su_own = sender.send(s_ref, rows_of(su_ref)(row), parts=-2)
+    su_own = sender.send(s_packed, su_blocks.at[row], parts=-2)
+
+    column, line = scales(pivot_ref[...])
+    x_ref[...] = newton(start_ref[...], rest_ref[...], 3)
+    rest = dot3(pivot_ref[...] * column * line, x_ref[...])
+    rest = jnp.where(eye(rest.shape[0]), 1.0 - rest, -rest) * flag_ref[0:1, 0:1]
+    g_ref[...] = (x_ref[...] + dot1(x_ref[...], rest)) * column * line
+
     from_below = [sender.send(upper(g_ref, i), upper(g_below, i), parts=1) for i in range(4)]
     from_above = [sender.send(upper(g_ref, i), upper(g_above, i), parts=-1) for i in range(4)]
     ring_next = Ring(sender, target)
@@ -279,7 +329,7 @@
     ring_w = Ring(sender, rows_of(wd_ref))
     ring_w.start()
     su_own.wait_recv()
-    ring_u = Ring(sender, rows_of(su_ref))
+    ring_u = Ring(sender, blocks_of(su_blocks))
     ring_u.start()
 
     @pl.when(odd)
@@ -294,7 +344,7 @@
         passed[3].start()
 
     v_from_below = sender.send(v_ref, v_below, parts=1)
-    sd_own = sender.send(s_ref, sdq_ref, parts=2)
+    sd_own = sender.send(s_packed, sdq_ref, parts=2)
     left_ref[...] = dot3(g_ref[...], v_ref[...])
 
     @pl.when(even)
@@ -335,6 +385,7 @@
     sd_own.wait_recv()
     ring_w.done()
     ring_u.done()
+    unpack(su_ref, su_blocks)
     sender.sent()
     v_from_above.wait_send()
     for ring in (ring_v, ring_w, ring_u):
@@ -351,16 +402,16 @@
     parts, g2_ref, v2_ref, u2_ref, left_ref, right_ref,
     above_left, above_right, below_right, wd_ref, su_ref, sdq_ref,
     s_out, y_out, down_in, up_in,
-    sd_ref, left2, c_ref, x_ref, y_ref, down_out, up_out,
+    sd_ref, sd_blocks, left2, c_ref, x_ref, y_ref, down_out, up_out,
     xs_out, ys_out, yd_out, xs_in, ys_in, yd_in, send_sems, recv_sems,
 ):
     sender = Sender(parts, send_sems, recv_sems)
     row = sender.row
     quarter = s_out.shape[0]
     own = pl.ds(pl.multiple_of(row * quarter, quarter), quarter)
-    sd_ref[own, :] = sdq_ref[...]
+    sd_blocks[row] = sdq_ref[...]
     sender.greet((0, 1), (0, -1), (1, 0), (-1, 0), (2, 0), (-2, 0))
-    ring_d = Ring(sender, rows_of(sd_ref))
+    ring_d = Ring(sender, blocks_of(sd_blocks))
     ring_d.start()
     c_ref[...] = dot3(v2_ref[...], wd_ref[...]) + dot3(u2_ref[...], su_ref[...])
     y_ref[...] = dot3(g2_ref[...], c_ref[...])
@@ -380,6 +431,7 @@
     c_ref[...] = dot3(g2_ref[...], x_ref[...])
     x_ref[...] = g2_ref[...] + dot3(c_ref[...], g2_ref[...])
     ring_d.done()
+    unpack(sd_ref, sd_blocks)
     c_ref[...] = dot3(left2[...], sd_ref[...])
     x_ref[...] = x_ref[...] + dot3(c_ref[...], left2[...], flip=True)
     xs_out[...] = dot3(above_left[...], x_ref[...]) - dot3(above_right[...], y_ref[...], flip=True)
@@ -421,19 +473,23 @@
             ),
         )(*operands)
 
+    packed = jax.ShapeDtypeStruct((3, quarter, quarter), f32)
+    packed_space = pltpu.VMEM((3, quarter, quarter), f32)
+    blocks_space = pltpu.VMEM((4, 3, quarter, quarter), f32)
     pivot = pivot_blocks[0]
-    g = inverse(inverse_kernel, pivot)
-    d2, x2, v2, u2, left, right, above_left, above_right, below_right, wd, su, sdq = call(
+    first = alone(begin_kernel, (whole, whole, jax.ShapeDtypeStruct((8, 128), f32)), pivot)
+    g, d2, x2, v2, u2, left, right, above_left, above_right, below_right, wd, su, sdq = call(
         second_kernel, 0,
-        (pivot, lower_blocks[0], top_diagonal[0], top_coupling[0], g),
-        [whole] * 6 + [strip] * 3 + [whole] * 2 + [strip],
-        [whole_space] * 2 + [strip_space] + [whole_space] * 6, 34,
+        (pivot, lower_blocks[0], top_diagonal[0], top_coupling[0]) + tuple(first),
+        [whole] * 7 + [strip] * 3 + [whole] * 2 + [packed],
+        [whole_space] * 2 + [strip_space, packed_space, blocks_space] + [whole_space] * 6, 34,
     )
-    g2 = inverse(finish_kernel, d2, x2)
+    g2 = alone(finish_kernel, whole, d2, x2)
     s, y, down, up = call(
         third_kernel, 1,
         (g2, v2, u2, left, right, above_left, above_right, below_right, wd, su, sdq),
-        [strip] * 4, [whole_space] * 5 + [strip_space] * 8, 9,
+        [strip] * 4,
+        [whole_space, blocks_space] + [whole_space] * 4 + [strip_space] * 8, 9,
     )
     start = lax.axis_index("rows") * quarter
     s = lax.dynamic_slice_in_dim(g, start, quarter, 0) + s

time: 84.1 us -> 80.5 us (0.957)
  Pallas kernels: 80.3 us -> 76.3 us
    pallas_call x2, Pallas kernels: 4.96 us -> 2.67 us  [alone(): pl.pallas_call(kernel, out_shape=results, in_specs=[VMEM] * len(operands)...]
    pallas_call x2, Pallas kernels: 75.4 us -> 73.6 us  [call(): pl.pallas_call(functools.partial(kernel, parts), out_shape=tuple(results)...]
where the time goes in v4:
time: 80.5 us; the launch traced here: 80 us
  Pallas kernels  76.3 us (95%)
  other arithmetic  1.63 us (2%)
  local copies, waits for them, and re-layouts  1.4 us (2%)
    pallas_call x2, Pallas kernels, call(): pl.pallas_call(functools.partial(kernel, parts), out_shape=tuple(results)...  73.6 us
    pallas_call x2, Pallas kernels, alone(): pl.pallas_call(kernel, out_shape=results, in_specs=[VMEM] * len(operands)...  2.67 us
    broadcast_in_dim x2, other arithmetic, local(): return (s[None], coupling[None], reduced[None])  1.63 us

profile of v4, /device:TPU:1, one launch (start us, length us, event | category | flops | bytes accessed | tf_op | source)
XLA Modules:
  0.0 80.0 jit_solution(16245596878006359466)
XLA Ops:
  0.6 0.0 copy-start
  0.6 1.2 %copy-done = f32[1,512,512]{2,1,0:T(8,128)S(1)} copy-done((f32[1,512,512]{2,1,0:T(8,128)S(1)}, f32[1,512,512]{2,1,0:T(8,128)}, u32[]{:S(2)}) %copy-start) | copy-done | bytes 1048600
  1.9 0.0 copy-start.1
  1.9 0.0 copy-start.2
  1.9 0.0 copy-start.3
  1.9 0.9 %shard_map.67 = (f32[512,512]{1,0:T(8,128)S(1)}, f32[512,512]{1,0:T(8,128)S(1)}, f32[8,128]{1,0:T(8,128)S(1)}) custom-call(f32[512,512]{1,0:T(8,128)S(1)} %bitcast.10), custom_call_target="tpu_custom_call" | custom-call | tf_op jit(solution)/shard_map/pallas_call | solution.py:132
  2.8 0.0 copy-done.1
  2.8 0.1 copy-done.2
  2.9 0.1 copy-done.3
  3.0 51.2 %shard_map.68 = (f32[512,512]{1,0:T(8,128)S(1)}, f32[512,512]{1,0:T(8,128)S(1)}, f32[512,512]{1,0:T(8,128)S(1)}, f32[512,512]{1,0:T(8,128)S(1)}, f32[512,512]{1,...) custom-call(f32[512,512]{1,0:T(8,128)S(1)} %bitcast.11, ...), custom_call_target="tpu_custom_call" | custom-call | tf_op jit(solution)/shard_map/pallas_call | solution.py:464
  54.2 1.8 %shard_map.69.g2_ref = f32[512,512]{1,0:T(8,128)S(1)} custom-call(f32[512,512]{1,0:T(8,128)S(1)} %get-tuple-element.27.pivot_ref, f32[512,512]{1,0:T(8,128)S(1)} %get-tuple-element.28.x_ref), custom_call_target="tpu_custom_call" | custom-call | tf_op jit(solution)/shard_map/pallas_call | solution.py:132
  55.9 22.4 %shard_map.70 = (f32[128,512]{1,0:T(8,128)S(1)}, f32[128,512]{1,0:T(8,128)S(1)}, f32[128,512]{1,0:T(8,128)S(1)}, f32[128,512]{1,0:T(8,128)S(1)}) custom-call(f32[512,512]{1,0:T(8,128)S(1)} %shard_map.69.g2_ref, f32[512,512]{1,0:T(8,128)S(1)} %get-tuple-element.29.v2_ref, f32[512,512]{1,0:T(8,128)S(1)} %get-tuple-element.30.u2_ref, ...), custom_call_target="tpu_custom_call" | custom-call | tf_op jit(solution)/shard_map/pallas_call | solution.py:464
  78.3 0.9 %subtract_bitcast_fusion = (f32[1,128,512]{2,1,0:T(8,128)}, f32[1,128,512]{2,1,0:T(8,128)}) fusion(f32[128,512]{1,0:T(8,128)S(1)} %get-tuple-element.42, f32[128,512]{1,0:T(8,128)S(1)} %get-tuple-element.41, f32[512,512]{1,0:T(8,128)S(1)} %get-tuple-element.27.pivot_ref, s32[]{:T(128)S(6)} %select_n.12, f32[128,512]{1,0:T(8,128)S(1)} %get-tuple-element.39, ...), kind=kLoop, calls=%fused_computation | loop fusion | flops 196608 | bytes 1835012 | tf_op jit(solution)/shard_map/broadcast_in_dim | solution.py:498
  79.2 0.7 select_bitcast_fusion
Async XLA Ops:
  0.6 1.2 %copy-start = (f32[1,512,512]{2,1,0:T(8,128)S(1)}, f32[1,512,512]{2,1,0:T(8,128)}, u32[]{:S(2)}) copy-start(f32[1,512,512]{2,1,0:T(8,128)} %param.4) | copy-start | bytes 3145732
  1.9 0.9 %copy-start.1 = (f32[1,512,128]{2,1,0:T(8,128)S(1)}, f32[1,512,128]{2,1,0:T(8,128)}, u32[]{:S(2)}) copy-start(f32[1,512,128]{2,1,0:T(8,128)} %param.5) | copy-start | bytes 786436
  1.9 1.0 %copy-start.2 = (f32[1,128,512]{2,1,0:T(8,128)S(1)}, f32[1,128,512]{2,1,0:T(8,128)}, u32[]{:S(2)}) copy-start(f32[1,128,512]{2,1,0:T(8,128)} %param.6) | copy-start | bytes 786436
  1.9 1.1 %copy-start.3 = (f32[1,128,512]{2,1,0:T(8,128)S(1)}, f32[1,128,512]{2,1,0:T(8,128)}, u32[]{:S(2)}) copy-start(f32[1,128,512]{2,1,0:T(8,128)} %param.7) | copy-start | bytes 786436

commit v5 on v4

--- a/solution.py
+++ b/solution.py
@@ -420,8 +420,7 @@
     left2[...] = dot3(g2_ref[...], v2_ref[...])
     down_out[...] = dot3(v2_ref[:, own].T, left2[...])
     from_above = sender.send(down_out, down_in, parts=-2)
-    x_ref[...] = dot3(g2_ref[...], u2_ref[...])
-    up_out[...] = dot3(u2_ref[:, own].T, x_ref[...])
+    up_out[...] = dot3(dot3(u2_ref[:, own].T, g2_ref[...]), u2_ref[...])
     from_below = sender.send(up_out, up_in, parts=2)
     x_ref[...] = dot3(u2_ref[...], wd_ref[...], flip=True)
     ring_d.forward()

time: 80.5 us -> 79.9 us (level)
  no operation moved by 1% of the time
where the time goes in v5:
time: 79.9 us; the launch traced here: 79.4 us
  Pallas kernels  75.7 us (95%)
  other arithmetic  1.63 us (2%)
  local copies, waits for them, and re-layouts  1.4 us (2%)
    pallas_call x2, Pallas kernels, call(): pl.pallas_call(functools.partial(kernel, parts), out_shape=tuple(results)...  73 us
    pallas_call x2, Pallas kernels, alone(): pl.pallas_call(kernel, out_shape=results, in_specs=[VMEM] * len(operands)...  2.67 us
    broadcast_in_dim x2, other arithmetic, local(): return (s[None], coupling[None], reduced[None])  1.63 us

profile of v5, /device:TPU:1, one launch (start us, length us, event | category | flops | bytes accessed | tf_op | source)
XLA Modules:
  0.0 79.4 jit_solution(17653413577457232175)
XLA Ops:
  0.6 0.0 copy-start
  0.6 1.2 %copy-done = f32[1,512,512]{2,1,0:T(8,128)S(1)} copy-done((f32[1,512,512]{2,1,0:T(8,128)S(1)}, f32[1,512,512]{2,1,0:T(8,128)}, u32[]{:S(2)}) %copy-start) | copy-done | bytes 1048600
  1.9 0.0 copy-start.1
  1.9 0.0 copy-start.2
  1.9 0.0 copy-start.3
  1.9 0.9 %shard_map.67 = (f32[512,512]{1,0:T(8,128)S(1)}, f32[512,512]{1,0:T(8,128)S(1)}, f32[8,128]{1,0:T(8,128)S(1)}) custom-call(f32[512,512]{1,0:T(8,128)S(1)} %bitcast.10), custom_call_target="tpu_custom_call" | custom-call | tf_op jit(solution)/shard_map/pallas_call | solution.py:132
  2.8 0.0 copy-done.1
  2.8 0.1 copy-done.2
  2.9 0.1 copy-done.3
  3.0 51.2 %shard_map.68 = (f32[512,512]{1,0:T(8,128)S(1)}, f32[512,512]{1,0:T(8,128)S(1)}, f32[512,512]{1,0:T(8,128)S(1)}, f32[512,512]{1,0:T(8,128)S(1)}, f32[512,512]{1,...) custom-call(f32[512,512]{1,0:T(8,128)S(1)} %bitcast.11, ...), custom_call_target="tpu_custom_call" | custom-call | tf_op jit(solution)/shard_map/pallas_call | solution.py:463
  54.2 1.8 %shard_map.69.g2_ref = f32[512,512]{1,0:T(8,128)S(1)} custom-call(f32[512,512]{1,0:T(8,128)S(1)} %get-tuple-element.27.pivot_ref, f32[512,512]{1,0:T(8,128)S(1)} %get-tuple-element.28.x_ref), custom_call_target="tpu_custom_call" | custom-call | tf_op jit(solution)/shard_map/pallas_call | solution.py:132
  55.9 21.8 %shard_map.70 = (f32[128,512]{1,0:T(8,128)S(1)}, f32[128,512]{1,0:T(8,128)S(1)}, f32[128,512]{1,0:T(8,128)S(1)}, f32[128,512]{1,0:T(8,128)S(1)}) custom-call(f32[512,512]{1,0:T(8,128)S(1)} %shard_map.69.g2_ref, f32[512,512]{1,0:T(8,128)S(1)} %get-tuple-element.29.v2_ref, f32[512,512]{1,0:T(8,128)S(1)} %get-tuple-element.30.u2_ref, ...), custom_call_target="tpu_custom_call" | custom-call | tf_op jit(solution)/shard_map/pallas_call | solution.py:463
  77.8 0.9 %subtract_bitcast_fusion = (f32[1,128,512]{2,1,0:T(8,128)}, f32[1,128,512]{2,1,0:T(8,128)}) fusion(f32[128,512]{1,0:T(8,128)S(1)} %get-tuple-element.42, f32[128,512]{1,0:T(8,128)S(1)} %get-tuple-element.41, f32[512,512]{1,0:T(8,128)S(1)} %get-tuple-element.27.pivot_ref, s32[]{:T(128)S(6)} %select_n.12, f32[128,512]{1,0:T(8,128)S(1)} %get-tuple-element.39, ...), kind=kLoop, calls=%fused_computation | loop fusion | flops 196608 | bytes 1835012 | tf_op jit(solution)/shard_map/broadcast_in_dim | solution.py:497
  78.7 0.7 select_bitcast_fusion
Async XLA Ops:
  0.6 1.2 %copy-start = (f32[1,512,512]{2,1,0:T(8,128)S(1)}, f32[1,512,512]{2,1,0:T(8,128)}, u32[]{:S(2)}) copy-start(f32[1,512,512]{2,1,0:T(8,128)} %param.4) | copy-start | bytes 3145732
  1.9 0.9 %copy-start.1 = (f32[1,512,128]{2,1,0:T(8,128)S(1)}, f32[1,512,128]{2,1,0:T(8,128)}, u32[]{:S(2)}) copy-start(f32[1,512,128]{2,1,0:T(8,128)} %param.5) | copy-start | bytes 786436
  1.9 1.0 %copy-start.2 = (f32[1,128,512]{2,1,0:T(8,128)S(1)}, f32[1,128,512]{2,1,0:T(8,128)}, u32[]{:S(2)}) copy-start(f32[1,128,512]{2,1,0:T(8,128)} %param.6) | copy-start | bytes 786436
  1.9 1.1 %copy-start.3 = (f32[1,128,512]{2,1,0:T(8,128)S(1)}, f32[1,128,512]{2,1,0:T(8,128)}, u32[]{:S(2)}) copy-start(f32[1,128,512]{2,1,0:T(8,128)} %param.7) | copy-start | bytes 786436
